TPU v7x, 32 devices: a whole 2x2x4 slice. The times are simulated.
32 devices in a mesh: dp: 8 (over z, y), mp: 4 (over x, core).
Axes of the slice: x: 2, y: 2, z: 4, core: 2. Of those that a mesh axis runs over, the one named last changes fastest.
Arguments:
- patches: bfloat16 [1152, 1024], P('mp', 'dp'), may hold values from -40 to 40
- counts: int32 [64], replicated, may hold values from 4 to 16, as said below
- dest: int32 [64], replicated, may hold values from 0 to 7, as said below
- w_qkv: bfloat16 [3, 1152, 1152], P(None, 'mp'), may hold values from -4 to 4
- w_out: bfloat16 [1152, 1152], P('mp'), may hold values from -0.1875 to 0.1875
- text: bfloat16 [64, 1152], P(('dp', 'mp')), may hold values from -6 to 6
Outputs:
- grad_image: float32 [64, 1152], P('dp', 'mp')
- grad_text: float32 [64, 1152], P(('dp', 'mp'))
Inputs may be any that keep to these rules, and one draw needn't show every extreme that they name: `counts`: every dp index holds 8 images; on some dp index every image that is sent to it has 16 patches. `dest`: entries s * 8 to s * 8 + 7 are a permutation of 0 to 7: every dp index sends exactly one image to every dp index.
All inputs are finite; a program needn't handle non-finite values.
Results may differ from a plain program's by a relative error of at most 0.0046.
Values may be sent and summed in bfloat16 or wider, within the bound.
No kernel may reach another device: no remote copies, remote signals or barrier semaphores. Data moves between devices by JAX's collectives and lax.ppermute only.
A program may use at most 64 MiB of HBM per device.

v0:
```python
import math

import jax
import jax.numpy as jnp
from jax import lax
from jax.sharding import PartitionSpec as P

D = 1152
HD = 72
MAXP = 16


def from_behind(shard, axis, by):
    peers = lax.axis_size(axis)
    return lax.ppermute(shard, axis, [(i, (i + by) % peers) for i in range(peers)])


def softmax_rounded(scores):
    row_max = jnp.max(scores, axis=-1, keepdims=True)
    raised = jnp.exp(scores - row_max)
    return (raised / jnp.sum(raised, axis=-1, keepdims=True)).astype(jnp.bfloat16)


def on_device(patches, counts, dest, w_qkv, w_out, text):
    devices = lax.axis_size("dp")
    lane_count = lax.axis_size("mp")
    dp_index = lax.axis_index("dp")
    mp_index = lax.axis_index("mp")
    width_local = patches.shape[0]
    heads_width = w_qkv.shape[1]
    heads_local = heads_width // HD
    count_table = counts.reshape(devices, devices)
    dest_table = dest.reshape(devices, devices)
    targets = jnp.arange(devices, dtype=jnp.int32)
    position = jnp.arange(MAXP, dtype=jnp.int32)
    own_counts = lax.dynamic_index_in_dim(count_table, dp_index, 0, keepdims=False)
    own_dest = lax.dynamic_index_in_dim(dest_table, dp_index, 0, keepdims=False)
    own_starts = jnp.cumsum(own_counts) - own_counts
    chosen = own_dest[None, :] == targets[:, None]
    send_count = jnp.sum(jnp.where(chosen, own_counts[None, :], 0), axis=1)
    send_start = jnp.sum(jnp.where(chosen, own_starts[None, :], 0), axis=1)
    send_valid = position[None, :] < send_count[:, None]
    send_rows = jnp.where(send_valid, send_start[:, None] + position[None, :], 0)
    picked = jnp.take(patches, send_rows.reshape(-1), axis=1).reshape(width_local, devices, MAXP)
    picked = jnp.where(send_valid[None, :, :], picked, jnp.zeros((), jnp.bfloat16))
    outgoing = jnp.transpose(picked, (1, 0, 2)).reshape(devices, width_local * MAXP)
    received = lax.all_to_all(outgoing, "dp", split_axis=0, concat_axis=0, tiled=True)
    arrived = dest_table == dp_index
    got_count = jnp.sum(jnp.where(arrived, count_table, 0), axis=1)
    got_index = jnp.sum(jnp.where(arrived, targets[None, :], 0), axis=1)
    image_ids = targets * devices + got_index
    counts_float = got_count.astype(jnp.float32)[:, None]
    rows_float = received.reshape(devices, width_local, MAXP).astype(jnp.float32)
    slice_mean = jnp.sum(rows_float, axis=2) / counts_float
    gathered = lax.all_gather(received, "mp", axis=1, tiled=True)
    full_float = gathered.reshape(devices, D, MAXP).astype(jnp.float32)
    row_mean = jnp.mean(full_float, axis=1, keepdims=True)
    centred = full_float - row_mean
    row_var = jnp.mean(centred * centred, axis=1, keepdims=True)
    normed = (centred * lax.rsqrt(row_var + 1e-06)).astype(jnp.bfloat16)
    projected = jnp.einsum("sdp,chd->csph", normed, w_qkv, preferred_element_type=jnp.float32)
    projected = projected.astype(jnp.bfloat16).reshape(3, devices, MAXP, heads_local, HD)
    query, key_rows, value = (projected[0], projected[1], projected[2])
    total_rows = devices * MAXP
    slot_ends = jnp.cumsum(got_count)
    slot_starts = slot_ends - got_count
    packed_row = jnp.arange(total_rows, dtype=jnp.int32)
    segment_of = jnp.sum((packed_row[:, None] >= slot_ends[None, :]).astype(jnp.int32), axis=1)
    live_row = packed_row < slot_ends[devices - 1]
    member = (segment_of[:, None] == targets[None, :]) & live_row[:, None]
    row_start = jnp.sum(jnp.where(member, slot_starts[None, :], 0), axis=1)
    source_row = jnp.where(live_row, segment_of * MAXP + packed_row - row_start, 0)
    segment_id = jnp.where(live_row, segment_of, -1)
    query_rows = query.reshape(total_rows, heads_local, HD)[source_row]
    key_packed = key_rows.reshape(total_rows, heads_local, HD)[source_row]
    value_packed = value.reshape(total_rows, heads_local, HD)[source_row]
    tile_rows = math.gcd(total_rows, 512)
    tile_count = total_rows // tile_rows
    window = min(tile_rows + 2 * MAXP, total_rows)

    def attend_tile(item):
        tile_index, query_tile, segment_tile = item
        window_start = jnp.clip(tile_index * tile_rows - MAXP, 0, total_rows - window)
        key_window = lax.dynamic_slice_in_dim(key_packed, window_start, window, 0)
        value_window = lax.dynamic_slice_in_dim(value_packed, window_start, window, 0)
        segment_window = lax.dynamic_slice_in_dim(segment_id, window_start, window, 0)
        scores = jnp.einsum(
            "phd,qhd->hpq", query_tile, key_window, preferred_element_type=jnp.float32
        ) / math.sqrt(HD)
        same_image = segment_tile[:, None] == segment_window[None, :]
        scores = jnp.where(same_image[None, :, :], scores, -1e30)
        weights = softmax_rounded(scores)
        return jnp.einsum(
            "hpq,qhd->phd", weights, value_window, preferred_element_type=jnp.float32
        ).astype(jnp.bfloat16)

    tile_numbers = jnp.arange(tile_count, dtype=jnp.int32)
    mixed = lax.map(
        attend_tile,
        (
            tile_numbers,
            query_rows.reshape(tile_count, tile_rows, heads_local, HD),
            segment_id.reshape(tile_count, tile_rows),
        ),
    )
    mixed = mixed.reshape(total_rows, heads_width)
    summed = jnp.einsum(
        "rs,rh->sh", member.astype(jnp.bfloat16), mixed, preferred_element_type=jnp.float32
    )
    pooled_heads = (summed / counts_float).astype(jnp.bfloat16)
    pool_term = jnp.dot(pooled_heads, w_out, preferred_element_type=jnp.float32)
    start_column = mp_index * width_local
    own_columns = lax.dynamic_slice_in_dim(pool_term, start_column, width_local, 1) + slice_mean
    pool_term = lax.dynamic_update_slice(
        pool_term, own_columns, (jnp.zeros((), jnp.int32), start_column)
    )
    pooled = lax.psum(pool_term, "mp")
    image_unit = (
        pooled * lax.rsqrt(jnp.sum(pooled * pooled, axis=-1, keepdims=True) + 1e-06)
    ).astype(jnp.bfloat16)
    text_float = text.astype(jnp.float32)
    text_unit = (
        text_float * lax.rsqrt(jnp.sum(text_float * text_float, axis=-1, keepdims=True) + 1e-06)
    ).astype(jnp.bfloat16)
    texts_here = text.shape[0]
    text_offsets = jnp.arange(texts_here, dtype=jnp.int32)

    def pair_turn(step_index, carried):
        travelling, text_grads, image_partial = carried
        anchor = (dp_index - step_index) % devices
        text_ids = (anchor * lane_count + mp_index) * texts_here + text_offsets
        travelling_bf = travelling.astype(jnp.bfloat16)
        logits = (
            4.0
            * jnp.einsum("ad,jd->aj", image_unit, travelling_bf, preferred_element_type=jnp.float32)
            - 2.0
        )
        labels = jnp.where(image_ids[:, None] == text_ids[None, :], 1.0, -1.0)
        dscaled = (-4.0 * labels * jax.nn.sigmoid(-labels * logits)).astype(jnp.bfloat16)
        image_partial = image_partial + jnp.einsum(
            "aj,jd->ad", dscaled, travelling_bf, preferred_element_type=jnp.float32
        )
        text_grads = text_grads + jnp.einsum(
            "aj,ad->jd", dscaled, image_unit, preferred_element_type=jnp.float32
        )
        travelling, text_grads = from_behind((travelling, text_grads), "dp", 1)
        return (travelling, text_grads, image_partial)

    initial = (
        text_unit.astype(jnp.float32),
        jnp.zeros((texts_here, D), jnp.float32),
        jnp.zeros((devices, D), jnp.float32),
    )
    travelling, text_grads, image_partial = lax.fori_loop(0, devices, pair_turn, initial)
    grad_image = lax.psum_scatter(image_partial, "mp", scatter_dimension=1, tiled=True)
    return (grad_image, text_grads)


def solution(mesh):
    placed = (P("mp", "dp"), P(), P(), P(None, "mp", None), P("mp", None), P(("dp", "mp"), None))
    return jax.shard_map(
        on_device,
        mesh=mesh,
        in_specs=placed,
        out_specs=(P("dp", "mp"), P(("dp", "mp"), None)),
        check_vma=False,
    )
```

profile of v0, /device:TPU:0, one launch (start us, length us, event | category | flops | bytes accessed | tf_op | source)
XLA Modules:
  0.0 156.9 jit_solution(18383174014571829487)
XLA Ops:
  7.2 0.9 reshape.266
  8.1 0.7 reshape.265
  9.2 0.6 slice.16
  10.3 0.7 iota_compare_fusion.4
  11.2 0.7 fusion.52
  11.8 1.0 copy.25
  12.8 0.9 gather_fusion
  13.7 0.3 copy.26
  14.1 0.4 all_to_all.11
  14.5 0.6 broadcast.255
  15.1 1.1 reduce.4
  16.2 0.6 reshape.312
  16.8 7.3 %all-to-all-start = ((bf16[8,2,2304]{2,1,0:T(2,128)(2,1)}), bf16[8,2,2304]{2,1,0:T(2,128)(2,1)S(1)}, u32[]{:S(2)}, u32[]{:S(2)}) async-start(bf16[8,2,2304]{2,1,0:T(2,128)(2,1)} %reshape.312), calls=%async_computation | async-start | bytes 147456 | tf_op jit(solution)/shard_map/all_to_all | solution.py:47
  24.2 0.7 broadcast_select_fusion
  24.8 0.8 fusion.40
  25.6 0.8 fusion.43
  26.5 4.5 %all-to-all-done = bf16[8,2,2304]{2,1,0:T(2,128)(2,1)S(1)} async-done(((bf16[8,2,2304]{2,1,0:T(2,128)(2,1)}), bf16[8,2,2304]{2,1,0:T(2,128)(2,1)S(1)}, u32[]{:S(2)}, u32[]{:S(2)}) %all-to-all-start) | async-done | bytes 73760 | tf_op jit(solution)/shard_map/all_to_all | solution.py:47
  31.2 0.4 convert_reduce_fusion.1
  31.6 7.5 %all-gather = bf16[8,1,18432]{2,1,0:T(2,128)(2,1)S(1)} all-gather(bf16[8,1,4608]{2,1,0:T(2,128)(2,1)S(1)} %reshape.313), channel_id=2, replica_groups=mesh['dp'=8,'mp'=4] {'mp'}, dimensions={2}, use_global_device_ids=true | all-gather | bytes 368640 | tf_op jit(solution)/shard_map/all_gather | solution.py:55
  39.1 2.5 %convert_reduce_fusion = f32[8,18432]{1,0:T(8,128)} fusion(bf16[8,1,18432]{2,1,0:T(2,128)(2,1)S(1)} %all-gather), kind=kLoop, calls=%fused_computation.40 | loop fusion | flops 147456 | bytes 884736 | tf_op jit(solution)/shard_map/convert_element_type | solution.py:56
  41.6 0.4 reshape.270
  42.0 4.8 %reshape.269 = f32[8,1152,16]{2,1,0:T(8,128)} reshape(f32[8,18432]{1,0:T(8,128)} %convert_reduce_fusion) | data formatting | bytes 1179648 | tf_op jit(solution)/shard_map/convert_element_type | solution.py:56
  46.7 0.5 reduce_sum.122
  47.2 2.7 %reduce_sum.117 = f32[8,16]{1,0:T(8,128)S(1)} reduce(f32[8,1152,16]{2,1,0:T(8,128)} %reshape.269, f32[]{:T(128)} %constant.181.clone.1), dimensions={1}, to_apply=%region_7.8 | reduce | flops 147328 | bytes 590340 | tf_op jit(solution)/shard_map/reduce_sum | solution.py:57
  49.9 3.1 %multiply_reduce_fusion = f32[8,16]{1,0:T(8,128)S(1)} fusion(f32[8,1152,16]{2,1,0:T(8,128)} %reshape.269, f32[8,16]{1,0:T(8,128)S(1)} %broadcast_multiply_fusion), kind=kLoop, calls=%fused_computation.24 | loop fusion | flops 442240 | bytes 590848 | tf_op jit(solution)/shard_map/reduce_sum | solution.py:59
  53.0 0.6 copy-done.1
  53.6 3.2 %fusion.27 = bf16[3,8,16,288]{3,2,0,1:T(8,128)(2,1)S(1)} fusion(bf16[3,288,1152]{2,1,0:T(8,128)(2,1)S(1)} %copy-done, f32[8,1152,16]{2,1,0:T(8,128)S(1)} %copy-done.1, f32[8,16]{1,0:T(8,128)S(1)} %add_rsqrt_fusion, f32[8,16]{1,0:T(8,128)S(1)} %broadcast_multiply_fusion), kind=kOutput, calls=%fused_computation.32 | convolution fusion | flops 255356928 | bytes 2802688 | tf_op jit(solution)/shard_map/sdp,chd->csph/dot_general | solution.py:61
  57.2 0.7 gather_fusion.2
  57.9 0.7 gather_fusion.3
  58.7 0.2 fusion.32
  59.1 0.7 gather_fusion.1
  59.9 0.2 convolution_convert_fusion
  60.1 0.3 fusion.35
  60.5 0.3 dynamic_update_slice.6
  60.8 11.1 %psum.7 = f32[8,1152]{1,0:T(8,128)S(1)} all-reduce(f32[8,1152]{1,0:T(8,128)S(1)} %dynamic_update_slice.6), channel_id=1, replica_groups=mesh['dp'=8,'mp'=4] {'mp'}, use_global_device_ids=true, to_apply=%region_13.14 | all-reduce | flops 9216 | bytes 73728 | tf_op jit(solution)/shard_map/psum | solution.py:117
  72.1 53.9 %while.24 = (s32[]{:T(128)}, bf16[2,1152]{1,0:T(2,128)(2,1)S(1)}, f32[2,1152]{1,0:T(2,128)S(1)}, f32[8,1152]{1,0:T(8,128)S(1)}, s32[8]{0:T(128)S(1)}, /*index=5*...) while((s32[]{:T(128)}, bf16[2,1152]{1,0:T(2,128)(2,1)S(1)}, ...), condition=%wide.region_17.18_spmd.clone, body=%wide.region_16.17_spmd.clone.sunk | while | flops 131540 | bytes 203280 | solution.py:154
  72.1 0.4 collective-permute-start
  72.8 1.3 collective-permute-start.1
  74.2 4.2 %collective-permute-done = bf16[2,1152]{1,0:T(2,128)(2,1)S(1)} collective-permute-done((bf16[2,1152]{1,0:T(2,128)(2,1)S(1)}, bf16[2,1152]{1,0:T(2,128)(2,1)S(1)}, u32[]{:S(2)}, u32[]{:S(2)}) %collective-permute-start) | collective-permute-done | bytes 4640 | tf_op jit(solution)/shard_map/while/body/eval_jaxpr/ppermute | solution.py:15
  78.4 0.7 collective-permute-done.1
  79.4 0.5 collective-permute-start.1
  80.1 5.3 %collective-permute-done = bf16[2,1152]{1,0:T(2,128)(2,1)S(1)} collective-permute-done((bf16[2,1152]{1,0:T(2,128)(2,1)S(1)}, bf16[2,1152]{1,0:T(2,128)(2,1)S(1)}, u32[]{:S(2)}, u32[]{:S(2)}) %collective-permute-start) | collective-permute-done | bytes 4640 | tf_op jit(solution)/shard_map/while/body/eval_jaxpr/ppermute | solution.py:15
  85.4 0.4 collective-permute-done.1
  86.1 0.2 convolution_add_fusion.5
  86.3 5.8 %collective-permute-done = bf16[2,1152]{1,0:T(2,128)(2,1)S(1)} collective-permute-done((bf16[2,1152]{1,0:T(2,128)(2,1)S(1)}, bf16[2,1152]{1,0:T(2,128)(2,1)S(1)}, u32[]{:S(2)}, u32[]{:S(2)}) %collective-permute-start) | collective-permute-done | bytes 4640 | tf_op jit(solution)/shard_map/while/body/eval_jaxpr/ppermute | solution.py:15
  92.1 0.4 collective-permute-done.1
  92.8 0.2 convolution_add_fusion.5
  93.0 5.8 %collective-permute-done = bf16[2,1152]{1,0:T(2,128)(2,1)S(1)} collective-permute-done((bf16[2,1152]{1,0:T(2,128)(2,1)S(1)}, bf16[2,1152]{1,0:T(2,128)(2,1)S(1)}, u32[]{:S(2)}, u32[]{:S(2)}) %collective-permute-start) | collective-permute-done | bytes 4640 | tf_op jit(solution)/shard_map/while/body/eval_jaxpr/ppermute | solution.py:15
  98.8 0.4 collective-permute-done.1
  99.5 0.2 convolution_add_fusion.5
  99.7 5.8 %collective-permute-done = bf16[2,1152]{1,0:T(2,128)(2,1)S(1)} collective-permute-done((bf16[2,1152]{1,0:T(2,128)(2,1)S(1)}, bf16[2,1152]{1,0:T(2,128)(2,1)S(1)}, u32[]{:S(2)}, u32[]{:S(2)}) %collective-permute-start) | collective-permute-done | bytes 4640 | tf_op jit(solution)/shard_map/while/body/eval_jaxpr/ppermute | solution.py:15
  105.5 0.4 collective-permute-done.1
  106.4 5.8 %collective-permute-done = bf16[2,1152]{1,0:T(2,128)(2,1)S(1)} collective-permute-done((bf16[2,1152]{1,0:T(2,128)(2,1)S(1)}, bf16[2,1152]{1,0:T(2,128)(2,1)S(1)}, u32[]{:S(2)}, u32[]{:S(2)}) %collective-permute-start) | collective-permute-done | bytes 4640 | tf_op jit(solution)/shard_map/while/body/eval_jaxpr/ppermute | solution.py:15
  112.2 0.4 collective-permute-done.1
  112.9 0.2 convolution_add_fusion.5
  113.1 5.8 %collective-permute-done = bf16[2,1152]{1,0:T(2,128)(2,1)S(1)} collective-permute-done((bf16[2,1152]{1,0:T(2,128)(2,1)S(1)}, bf16[2,1152]{1,0:T(2,128)(2,1)S(1)}, u32[]{:S(2)}, u32[]{:S(2)}) %collective-permute-start) | collective-permute-done | bytes 4640 | tf_op jit(solution)/shard_map/while/body/eval_jaxpr/ppermute | solution.py:15
  118.9 0.4 collective-permute-done.1
  119.6 0.2 convolution_add_fusion.5
  119.8 5.8 %collective-permute-done = bf16[2,1152]{1,0:T(2,128)(2,1)S(1)} collective-permute-done((bf16[2,1152]{1,0:T(2,128)(2,1)S(1)}, bf16[2,1152]{1,0:T(2,128)(2,1)S(1)}, u32[]{:S(2)}, u32[]{:S(2)}) %collective-permute-start) | collective-permute-done | bytes 4640 | tf_op jit(solution)/shard_map/while/body/eval_jaxpr/ppermute | solution.py:15
  125.6 0.4 collective-permute-done.1
  125.9 1.0 copy.37
  127.0 20.9 %reduce-scatter.4.cloned.1.call-done = f32[288,8]{1,0:T(8,128)} async-done(((f32[1152,8]{1,0:T(8,128)}), f32[288,8]{1,0:T(8,128)}) %reduce-scatter.4.cloned.1.call-update) | async-done | bytes 9232
  147.9 1.6 %copy.38 = f32[8,288]{1,0:T(8,128)} copy(f32[8,288]{0,1:T(8,128)} %bitcast.90) | data formatting | bytes 18432
  149.5 0.6 copy.59
  (89 shorter events, 5.0 us)
Async XLA Ops:
  7.2 45.9 %copy-start = (bf16[3,288,1152]{2,1,0:T(8,128)(2,1)S(1)}, bf16[3,288,1152]{2,1,0:T(8,128)(2,1)}, u32[]{:S(2)}) copy-start(bf16[3,288,1152]{2,1,0:T(8,128)(2,1)} %param.11) | copy-start | bytes 5971972
  16.8 14.2 %all-to-all-start = ((bf16[8,2,2304]{2,1,0:T(2,128)(2,1)}), bf16[8,2,2304]{2,1,0:T(2,128)(2,1)S(1)}, u32[]{:S(2)}, u32[]{:S(2)}) async-start(bf16[8,2,2304]{2,1,0:T(2,128)(2,1)} %reshape.312), calls=%async_computation | async-start | bytes 147456 | tf_op jit(solution)/shard_map/all_to_all | solution.py:47
  24.1 123.7 %reduce-scatter.4.cloned.1.call-start = ((), (), s32[]{:S(2)}) async-start(), calls=%async_computation.2 | async-start | bytes 737280
  49.9 3.8 %copy-start.1 = (f32[8,1152,16]{2,1,0:T(8,128)S(1)}, f32[8,1152,16]{2,1,0:T(8,128)}, u32[]{:S(2)}) copy-start(f32[8,1152,16]{2,1,0:T(8,128)} %reshape.269) | copy-start | bytes 1769476
  53.6 6.5 %copy-start.2 = (bf16[288,1152]{1,0:T(8,128)(2,1)S(1)}, bf16[288,1152]{1,0:T(8,128)(2,1)}, u32[]{:S(2)}) copy-start(bf16[288,1152]{1,0:T(8,128)(2,1)} %param.12) | copy-start | bytes 1990660
  72.1 6.4 %collective-permute-start = (bf16[2,1152]{1,0:T(2,128)(2,1)S(1)}, bf16[2,1152]{1,0:T(2,128)(2,1)S(1)}, u32[]{:S(2)}, u32[]{:S(2)}) collective-permute-start(bf16[2,1152]{1,0:T(2,128)(2,1)S(1)} %copy.51), channel_id=1, source_target_pairs={{0,4},{4,8},{8,12},{12,16},{16,20},{20,24},{24,28},{28,0},{1,5},{5... | collective-permute-start | bytes 13832 | tf_op jit(solution)/shard_map/while/body/eval_jaxpr/ppermute | solution.py:15
  72.8 6.4 %collective-permute-start.1 = (f32[2,1152]{1,0:T(2,128)S(1)}, f32[2,1152]{1,0:T(2,128)S(1)}, u32[]{:S(2)}, u32[]{:S(2)}) collective-permute-start(f32[2,1152]{1,0:T(2,128)S(1)} %convolution_add_fusion.4), channel_id=1, source_target_pairs={{0,4},{4,8},{8,12},{12,16},{16,20},{20,24},{24,28},{28,0},{1,5},{5... | collective-permute-start | bytes 27656 | tf_op jit(solution)/shard_map/while/body/eval_jaxpr/ppermute | solution.py:15
  79.1 6.3 %collective-permute-start = (bf16[2,1152]{1,0:T(2,128)(2,1)S(1)}, bf16[2,1152]{1,0:T(2,128)(2,1)S(1)}, u32[]{:S(2)}, u32[]{:S(2)}) collective-permute-start(bf16[2,1152]{1,0:T(2,128)(2,1)S(1)} %copy.51), channel_id=1, source_target_pairs={{0,4},{4,8},{8,12},{12,16},{16,20},{20,24},{24,28},{28,0},{1,5},{5... | collective-permute-start | bytes 13832 | tf_op jit(solution)/shard_map/while/body/eval_jaxpr/ppermute | solution.py:15
  79.4 6.4 %collective-permute-start.1 = (f32[2,1152]{1,0:T(2,128)S(1)}, f32[2,1152]{1,0:T(2,128)S(1)}, u32[]{:S(2)}, u32[]{:S(2)}) collective-permute-start(f32[2,1152]{1,0:T(2,128)S(1)} %convolution_add_fusion.4), channel_id=1, source_target_pairs={{0,4},{4,8},{8,12},{12,16},{16,20},{20,24},{24,28},{28,0},{1,5},{5... | collective-permute-start | bytes 27656 | tf_op jit(solution)/shard_map/while/body/eval_jaxpr/ppermute | solution.py:15
  85.8 6.3 %collective-permute-start = (bf16[2,1152]{1,0:T(2,128)(2,1)S(1)}, bf16[2,1152]{1,0:T(2,128)(2,1)S(1)}, u32[]{:S(2)}, u32[]{:S(2)}) collective-permute-start(bf16[2,1152]{1,0:T(2,128)(2,1)S(1)} %copy.51), channel_id=1, source_target_pairs={{0,4},{4,8},{8,12},{12,16},{16,20},{20,24},{24,28},{28,0},{1,5},{5... | collective-permute-start | bytes 13832 | tf_op jit(solution)/shard_map/while/body/eval_jaxpr/ppermute | solution.py:15
  86.1 6.4 %collective-permute-start.1 = (f32[2,1152]{1,0:T(2,128)S(1)}, f32[2,1152]{1,0:T(2,128)S(1)}, u32[]{:S(2)}, u32[]{:S(2)}) collective-permute-start(f32[2,1152]{1,0:T(2,128)S(1)} %convolution_add_fusion.4), channel_id=1, source_target_pairs={{0,4},{4,8},{8,12},{12,16},{16,20},{20,24},{24,28},{28,0},{1,5},{5... | collective-permute-start | bytes 27656 | tf_op jit(solution)/shard_map/while/body/eval_jaxpr/ppermute | solution.py:15
  92.5 6.3 %collective-permute-start = (bf16[2,1152]{1,0:T(2,128)(2,1)S(1)}, bf16[2,1152]{1,0:T(2,128)(2,1)S(1)}, u32[]{:S(2)}, u32[]{:S(2)}) collective-permute-start(bf16[2,1152]{1,0:T(2,128)(2,1)S(1)} %copy.51), channel_id=1, source_target_pairs={{0,4},{4,8},{8,12},{12,16},{16,20},{20,24},{24,28},{28,0},{1,5},{5... | collective-permute-start | bytes 13832 | tf_op jit(solution)/shard_map/while/body/eval_jaxpr/ppermute | solution.py:15
  92.8 6.4 %collective-permute-start.1 = (f32[2,1152]{1,0:T(2,128)S(1)}, f32[2,1152]{1,0:T(2,128)S(1)}, u32[]{:S(2)}, u32[]{:S(2)}) collective-permute-start(f32[2,1152]{1,0:T(2,128)S(1)} %convolution_add_fusion.4), channel_id=1, source_target_pairs={{0,4},{4,8},{8,12},{12,16},{16,20},{20,24},{24,28},{28,0},{1,5},{5... | collective-permute-start | bytes 27656 | tf_op jit(solution)/shard_map/while/body/eval_jaxpr/ppermute | solution.py:15
  99.2 6.3 %collective-permute-start = (bf16[2,1152]{1,0:T(2,128)(2,1)S(1)}, bf16[2,1152]{1,0:T(2,128)(2,1)S(1)}, u32[]{:S(2)}, u32[]{:S(2)}) collective-permute-start(bf16[2,1152]{1,0:T(2,128)(2,1)S(1)} %copy.51), channel_id=1, source_target_pairs={{0,4},{4,8},{8,12},{12,16},{16,20},{20,24},{24,28},{28,0},{1,5},{5... | collective-permute-start | bytes 13832 | tf_op jit(solution)/shard_map/while/body/eval_jaxpr/ppermute | solution.py:15
  99.5 6.4 %collective-permute-start.1 = (f32[2,1152]{1,0:T(2,128)S(1)}, f32[2,1152]{1,0:T(2,128)S(1)}, u32[]{:S(2)}, u32[]{:S(2)}) collective-permute-start(f32[2,1152]{1,0:T(2,128)S(1)} %convolution_add_fusion.4), channel_id=1, source_target_pairs={{0,4},{4,8},{8,12},{12,16},{16,20},{20,24},{24,28},{28,0},{1,5},{5... | collective-permute-start | bytes 27656 | tf_op jit(solution)/shard_map/while/body/eval_jaxpr/ppermute | solution.py:15
  105.9 6.3 %collective-permute-start = (bf16[2,1152]{1,0:T(2,128)(2,1)S(1)}, bf16[2,1152]{1,0:T(2,128)(2,1)S(1)}, u32[]{:S(2)}, u32[]{:S(2)}) collective-permute-start(bf16[2,1152]{1,0:T(2,128)(2,1)S(1)} %copy.51), channel_id=1, source_target_pairs={{0,4},{4,8},{8,12},{12,16},{16,20},{20,24},{24,28},{28,0},{1,5},{5... | collective-permute-start | bytes 13832 | tf_op jit(solution)/shard_map/while/body/eval_jaxpr/ppermute | solution.py:15
  106.2 6.4 %collective-permute-start.1 = (f32[2,1152]{1,0:T(2,128)S(1)}, f32[2,1152]{1,0:T(2,128)S(1)}, u32[]{:S(2)}, u32[]{:S(2)}) collective-permute-start(f32[2,1152]{1,0:T(2,128)S(1)} %convolution_add_fusion.4), channel_id=1, source_target_pairs={{0,4},{4,8},{8,12},{12,16},{16,20},{20,24},{24,28},{28,0},{1,5},{5... | collective-permute-start | bytes 27656 | tf_op jit(solution)/shard_map/while/body/eval_jaxpr/ppermute | solution.py:15
  112.6 6.3 %collective-permute-start = (bf16[2,1152]{1,0:T(2,128)(2,1)S(1)}, bf16[2,1152]{1,0:T(2,128)(2,1)S(1)}, u32[]{:S(2)}, u32[]{:S(2)}) collective-permute-start(bf16[2,1152]{1,0:T(2,128)(2,1)S(1)} %copy.51), channel_id=1, source_target_pairs={{0,4},{4,8},{8,12},{12,16},{16,20},{20,24},{24,28},{28,0},{1,5},{5... | collective-permute-start | bytes 13832 | tf_op jit(solution)/shard_map/while/body/eval_jaxpr/ppermute | solution.py:15
  112.9 6.4 %collective-permute-start.1 = (f32[2,1152]{1,0:T(2,128)S(1)}, f32[2,1152]{1,0:T(2,128)S(1)}, u32[]{:S(2)}, u32[]{:S(2)}) collective-permute-start(f32[2,1152]{1,0:T(2,128)S(1)} %convolution_add_fusion.4), channel_id=1, source_target_pairs={{0,4},{4,8},{8,12},{12,16},{16,20},{20,24},{24,28},{28,0},{1,5},{5... | collective-permute-start | bytes 27656 | tf_op jit(solution)/shard_map/while/body/eval_jaxpr/ppermute | solution.py:15
  119.2 6.3 %collective-permute-start = (bf16[2,1152]{1,0:T(2,128)(2,1)S(1)}, bf16[2,1152]{1,0:T(2,128)(2,1)S(1)}, u32[]{:S(2)}, u32[]{:S(2)}) collective-permute-start(bf16[2,1152]{1,0:T(2,128)(2,1)S(1)} %copy.51), channel_id=1, source_target_pairs={{0,4},{4,8},{8,12},{12,16},{16,20},{20,24},{24,28},{28,0},{1,5},{5... | collective-permute-start | bytes 13832 | tf_op jit(solution)/shard_map/while/body/eval_jaxpr/ppermute | solution.py:15
  119.6 6.4 %collective-permute-start.1 = (f32[2,1152]{1,0:T(2,128)S(1)}, f32[2,1152]{1,0:T(2,128)S(1)}, u32[]{:S(2)}, u32[]{:S(2)}) collective-permute-start(f32[2,1152]{1,0:T(2,128)S(1)} %convolution_add_fusion.4), channel_id=1, source_target_pairs={{0,4},{4,8},{8,12},{12,16},{16,20},{20,24},{24,28},{28,0},{1,5},{5... | collective-permute-start | bytes 27656 | tf_op jit(solution)/shard_map/while/body/eval_jaxpr/ppermute | solution.py:15
Sparse Core Ops, SparseCore 0:
  127.1 20.6 reduce-scatter.3
where the time goes:
time: 157 us
  waiting for transfers between devices  73 us (46%)
  blocking collectives  18.6 us (12%)
  local copies, waits for them, and re-layouts  18.1 us (12%)
  other arithmetic  15.4 us (10%)
  between operations  14.3 us (9%)
  starting transfers between devices  9.54 us (6%)
  matrix products  7.65 us (5%)
    ppermute x16, waiting for transfers between devices, from_behind(): lax.ppermute(shard, axis, [(i, (i + by) % peers) for i in range(peers)])  47.6 us
    unnamed x2, waiting for transfers between devices  20.9 us
    psum x1, blocking collectives, on_device(): pooled = lax.psum(pool_term, 'mp')  11.1 us
    all_gather x1, blocking collectives, on_device(): gathered = lax.all_gather(received, 'mp', axis=1, tiled=True)  7.53 us
    all_to_all x1, starting transfers between devices, on_device(): lax.all_to_all(outgoing, 'dp', split_axis=0, concat_axis=0, tiled=True)  7.28 us
    unnamed x12, local copies, waits for them, and re-layouts  5.56 us
    convert_element_type x1, local copies, waits for them, and re-layouts, on_device(): full_float = gathered.reshape(devices, D, MAXP).astype(jnp.float32)  4.77 us
    all_to_all x1, waiting for transfers between devices, on_device(): lax.all_to_all(outgoing, 'dp', split_axis=0, concat_axis=0, tiled=True)  4.54 us
  transfers between devices with their start and end apart: 18, of which 18 were waited for; matrix products, arithmetic and copies ran while one was open for 4% of the time, Pallas kernels for 0%

commit v1 on v0

v1 whole, which is shorter than its diff:
```python
import functools
import math

import jax
import jax.numpy as jnp
from jax import lax
from jax.experimental import pallas as pl
from jax.experimental.pallas import tpu as pltpu
from jax.sharding import PartitionSpec as P

HD = 72
EPS = 1e-06
F32 = jnp.float32
BF16 = jnp.bfloat16
LAST_LAST = (((1,), (1,)), ((), ()))
FIRST_FIRST = (((0,), (0,)), ((), ()))


def dot(lhs, rhs, dims=(((1,), (0,)), ((), ()))):
    return lax.dot_general(lhs, rhs, dims, preferred_element_type=F32)


def iota(shape, dim):
    return lax.broadcasted_iota(jnp.int32, shape, dim)


def digits_of(peers):
    digits, stride = [], 1
    for factor in (2, 4, 3):
        while peers % factor == 0 and (factor != 2 or peers % 4):
            digits.append((stride, factor))
            stride, peers = stride * factor, peers // factor
    if peers > 1:
        digits.append((stride, peers))
    return digits[::-1]


def shifted(index, stride, radix, by):
    digit = index // stride % radix
    new = (digit + by) % radix if radix & (radix - 1) else digit ^ by
    return index + (new - digit) * stride


def moved(index, position, digits):
    place = 1
    for stride, radix in digits:
        index = shifted(index, stride, radix, position // place % radix)
        place *= radix
    return index


def fetch(block, axis, stride, radix, by):
    peers = lax.axis_size(axis)
    return lax.ppermute(block, axis, [(shifted(i, stride, radix, by), i) for i in range(peers)])


def load(images, *refs):
    sources, refs = refs[:6], refs[6:]
    *here, bias, member, spread, chosen, counts, dest, sems = refs
    copies = [
        pltpu.make_async_copy(source, target, sems.at[index])
        for index, (source, target) in enumerate(zip(sources, [counts, dest, *here]))
    ]
    for copy in copies:
        copy.start()
    for copy in copies[:2]:
        copy.wait()
    dp_index = lax.axis_index("dp")
    devices = chosen.shape[0]
    rows = member.shape[1]

    ends = []
    total = jnp.int32(0)
    for image in range(images):
        total = total + counts[dp_index * images + image]
        ends.append(total)

    def image_of(position):
        index = jnp.zeros(position.shape, jnp.int32)
        for end in ends:
            index = index + (position >= end).astype(jnp.int32)
        return index

    image_of_lane = image_of(iota((1, rows), 1))
    image_of_sublane = image_of(iota((rows, 1), 0))
    bias[...] = jnp.where(image_of_sublane == image_of_lane, 0.0, -1e30)
    belongs = (iota((images, rows), 0) == image_of_lane).astype(F32)
    member[...] = belongs
    heads = spread.shape[0] // images
    for head in range(heads):
        blocks = [belongs if other == head else jnp.zeros_like(belongs) for other in range(heads)]
        spread[head * images : (head + 1) * images, :] = jnp.concatenate(blocks, axis=1)

    target = moved(dp_index, iota((devices, images), 0), digits_of(devices))
    image = iota((devices, images), 1)
    goes = jnp.zeros((devices, images), F32)
    for index in range(images):
        here = (image == index) & (target == dest[dp_index * images + index])
        goes = jnp.where(here, 1.0, goes)
    chosen[...] = goes
    for copy in copies[2:]:
        copy.wait()


def attend(offsets, *refs):
    lanes = len(offsets)
    *pieces, bias, member, spread, w_qkv, w_out, share, patch_mean, x_rows = refs
    mp_index = lax.axis_index("mp")
    piece_width = pieces[0].shape[0]
    width, rows = x_rows.shape
    images = share.shape[0]
    local = w_qkv.shape[1]
    heads = local // HD

    for offset, piece in zip(offsets, pieces):
        start = moved(mp_index, offset, digits_of(lanes)) * piece_width
        x_rows[pl.ds(pl.multiple_of(start, 8), piece_width), :] = piece[...].astype(F32)
    x = x_rows[...]
    centred = x - jnp.sum(x, axis=0, keepdims=True) * (1.0 / width)
    variance = jnp.sum(centred * centred, axis=0, keepdims=True) * (1.0 / width)
    normed = (centred * lax.rsqrt(variance + EPS)).astype(BF16)
    query, key, value = (dot(w_qkv[which], normed) for which in range(3))

    belongs = member[...]
    count = jnp.sum(belongs, axis=1, keepdims=True)
    patch_mean[...] = dot(belongs.astype(BF16), x.astype(BF16), LAST_LAST) / count
    queries = []
    for head in range(heads):
        above, below = head * HD, (heads - 1 - head) * HD
        own = query[above : above + HD]
        blocks = [jnp.zeros((above, rows), F32)] * (above > 0) + [own]
        blocks += [jnp.zeros((below, rows), F32)] * (below > 0)
        queries.append(jnp.concatenate(blocks, axis=0))
    queries = jnp.concatenate(queries, axis=1).astype(BF16)
    scores = dot(key.T.astype(BF16), queries) * (1.0 / math.sqrt(HD))
    scores = scores + jnp.concatenate([bias[...]] * heads, axis=1)
    raised = jnp.exp(scores - jnp.max(scores, axis=0, keepdims=True))
    weights = (raised * (1.0 / jnp.sum(raised, axis=0, keepdims=True))).astype(BF16)
    pooling = dot(spread[...].astype(BF16), weights, LAST_LAST).astype(BF16)
    mixed = dot(pooling, value.astype(BF16), LAST_LAST)
    column_head = iota((images, local), 1) // HD
    pooled_heads = jnp.zeros((images, local), F32)
    for head in range(heads):
        block = mixed[head * images : (head + 1) * images]
        pooled_heads = jnp.where(column_head == head, block, pooled_heads)
    pooled_heads = (pooled_heads / count).astype(BF16)
    share[...] = dot(pooled_heads, w_out[...])


def join(*refs):
    first, *texts, share, message = refs
    texts = [first, *texts[::-1]]
    text = jnp.concatenate([text[...].astype(F32) for text in texts], axis=0)
    text = text * lax.rsqrt(jnp.sum(text * text, axis=1, keepdims=True) + EPS)
    message[...] = jnp.concatenate([text, share[...]], axis=0).astype(BF16)


def pair(lanes, *refs):
    chosen, patch_mean, share, own, *others, message = refs
    arrived = [own, *others[::-1]]
    devices = message.shape[0]
    dp_index = lax.axis_index("dp")
    mp_index = lax.axis_index("mp")
    images, width = patch_mean.shape
    group = arrived[0].shape[0] - images
    texts_here = group // devices
    slice_width = width // lanes
    part = message.shape[2] - width

    pooled = patch_mean[...] + share[...]
    for block in arrived[1:]:
        pooled = pooled + block[...].astype(F32)[group:]
    image_unit = (
        pooled * lax.rsqrt(jnp.sum(pooled * pooled, axis=1, keepdims=True) + EPS)
    ).astype(BF16)
    text_unit = jnp.concatenate([block[:group] for block in arrived], axis=0)

    def scaled(logits, image_dim, text_dim):
        image_id = dp_index * images + iota(logits.shape, image_dim)
        index = iota(logits.shape, text_dim)
        text_dp = moved(dp_index, index % group // texts_here, digits_of(devices))
        text_mp = moved(mp_index, index // group, digits_of(lanes))
        text_id = (text_dp * lanes + text_mp) * texts_here + index % texts_here
        label = jnp.where(image_id == text_id, 1.0, -1.0)
        logits = 4.0 * logits - 2.0
        return -4.0 * label * jax.nn.sigmoid(-label * logits)

    by_image = scaled(dot(image_unit, text_unit, LAST_LAST), 0, 1)
    by_text = scaled(dot(text_unit[:group], image_unit, LAST_LAST), 1, 0).astype(BF16)

    goes = chosen[...]
    rows = sum(goes[:, image : image + 1] * by_image[image : image + 1] for image in range(images))
    image_grad = dot(rows.astype(BF16), text_unit)
    own_columns = image_grad[:, :slice_width]
    for lane in range(1, lanes):
        block = image_grad[:, lane * slice_width : (lane + 1) * slice_width]
        own_columns = jnp.where(mp_index == lane, block, own_columns)
    text_grad = dot(by_text, image_unit)
    parts = [own_columns[:, which * part : (which + 1) * part] for which in range(texts_here)]
    for position in range(devices):
        first = position * texts_here
        row = [block[position : position + 1] for block in parts]
        both = [text_grad[first : first + texts_here], jnp.concatenate(row, axis=0)]
        target = moved(dp_index, position, digits_of(devices))
        message[target] = jnp.concatenate(both, axis=1).astype(BF16)


def collect(message, image_grad, text_grad):
    texts_here, width = text_grad.shape
    part = message.shape[2] - width
    arrived = message[...].astype(F32)
    text_grad[...] = jnp.sum(arrived[:, :, :width], axis=0)
    for which in range(texts_here):
        columns = slice(which * part, (which + 1) * part)
        for source in range(arrived.shape[0]):
            image_grad[source : source + 1, columns] = arrived[source, which : which + 1, width:]


def call(kernel, out_shape, args, spaces=None, scratch=(), cost=None):
    spaces = spaces or [pltpu.VMEM] * len(args)
    return pl.pallas_call(
        kernel,
        out_shape=out_shape,
        in_specs=[pl.BlockSpec(memory_space=space) for space in spaces],
        out_specs=jax.tree.map(lambda _: pl.BlockSpec(memory_space=pltpu.VMEM), out_shape),
        scratch_shapes=scratch,
        cost_estimate=cost,
        compiler_params=pltpu.CompilerParams(vmem_limit_bytes=32 * 2**20),
    )(*args)


def on_device(patches, counts, dest, w_qkv, w_out, text):
    devices = lax.axis_size("dp")
    lanes = lax.axis_size("mp")
    images = counts.shape[0] // devices
    width = w_qkv.shape[2]
    rows = patches.shape[1]
    texts_here = text.shape[0]
    slice_width = width // lanes
    heads = w_qkv.shape[1] // HD
    dp_digits, mp_digits = digits_of(devices), digits_of(lanes)
    shape = jax.ShapeDtypeStruct

    sources = [counts, dest, patches, w_qkv, w_out, text]
    patches_here, w_qkv_here, w_out_here, text_here, bias, member, spread, chosen = call(
        functools.partial(load, images),
        (
            *(shape(source.shape, source.dtype) for source in sources[2:]),
            shape((rows, rows), F32),
            shape((images, rows), F32),
            shape((heads * images, heads * rows), F32),
            shape((devices, images), F32),
        ),
        [pltpu.with_memory_space_constraint(source, pltpu.HBM) for source in sources],
        [pltpu.HBM] * 6,
        scratch=[
            pltpu.SMEM(counts.shape, jnp.int32),
            pltpu.SMEM(dest.shape, jnp.int32),
            pltpu.SemaphoreType.DMA((6,)),
        ],
        cost=pl.CostEstimate(flops=0, bytes_accessed=6 * w_qkv.size, transcendentals=0),
    )

    offsets = range(lanes)
    pieces = [
        lax.ppermute(patches, "mp", [(moved(i, offset, mp_digits), i) for i in range(lanes)])
        for offset in offsets[1:]
    ]
    texts = [text_here]
    for stride, radix in dp_digits:
        block = jnp.concatenate(texts, axis=0)
        sent = block if len(texts) > 1 else text
        texts = [block] + [fetch(sent, "dp", stride, radix, by) for by in range(1, radix)]

    share, patch_mean = call(
        functools.partial(attend, offsets),
        (shape((images, width), F32), shape((images, width), F32)),
        [patches_here, *pieces, bias, member, spread, w_qkv_here, w_out_here],
        scratch=[pltpu.VMEM((width, rows), F32)],
    )
    texts = [texts[0], *texts[:0:-1]]
    message = call(join, shape((devices * texts_here + images, width), BF16), [*texts, share])
    arrived = [message] + [
        lax.ppermute(message, "mp", [(moved(i, offset, mp_digits), i) for i in range(lanes)])
        for offset in offsets[1:]
    ]
    message = call(
        functools.partial(pair, lanes),
        shape((devices, texts_here, width + slice_width // texts_here), BF16),
        [chosen, patch_mean, share, arrived[0], *arrived[:0:-1]],
    )
    message = lax.all_to_all(message, "dp", split_axis=0, concat_axis=0, tiled=True)
    return call(
        collect,
        (shape((devices, slice_width), F32), shape((texts_here, width), F32)),
        [message],
    )


def solution(mesh):
    placed = (P("mp", "dp"), P(), P(), P(None, "mp", None), P("mp", None), P(("dp", "mp"), None))
    return jax.shard_map(
        on_device,
        mesh=mesh,
        in_specs=placed,
        out_specs=(P("dp", "mp"), P(("dp", "mp"), None)),
        check_vma=False,
    )
```

time: 157 us -> 32.2 us (0.21)
  waiting for transfers between devices: 73 us -> 4.86 us
  local copies, waits for them, and re-layouts: 18.1 us -> 0 us
  other arithmetic: 15.4 us -> 0.02 us
  between operations: 14.3 us -> 0.68 us
  blocking collectives: 18.6 us -> 9.91 us
  matrix products: 7.65 us -> 0 us
  Pallas kernels: 0 us -> 5.11 us
  starting transfers between devices: 9.54 us -> 11.4 us
    ppermute x16 -> x10, waiting for transfers between devices: 47.6 us -> 4.86 us  [the longest x3 3.45 us: on_device(): lax.ppermute(message, 'mp', [(moved(i, offset, mp_digits), i) for i in ra...]
    unnamed x2 -> x0, waiting for transfers between devices: 20.9 us -> none
    psum x1 -> x0, blocking collectives: 11.1 us -> none  [on_device(): pooled = lax.psum(pool_term, 'mp')]
    all_to_all x0 -> x1, blocking collectives: none -> 9.91 us  [on_device(): lax.all_to_all(message, 'dp', split_axis=0, concat_axis=0, tiled=True)]
    ppermute x16 -> x10, starting transfers between devices: 2.22 us -> 11.4 us  [the longest x4 7.66 us: fetch(): lax.ppermute(block, axis, [(shifted(i, stride, radix, by), i) for i in ra...]
    dot_general x28 -> x0, matrix products: 7.65 us -> none  [the longest x1 3.24 us: on_device(): jnp.einsum('sdp,chd->csph', normed, w_qkv, preferred_element_type=jnp.flo...]
    reduce_sum x9 -> x0, other arithmetic: 7.64 us -> none  [the longest x1 3.12 us: on_device(): row_var = jnp.mean(centred * centred, axis=1, keepdims=True)]
    all_gather x1 -> x0, blocking collectives: 7.53 us -> none  [on_device(): gathered = lax.all_gather(received, 'mp', axis=1, tiled=True)]
  transfers between devices with their start and end apart: 18 -> 10, of which waited for: 18 -> 4; matrix products, arithmetic and copies ran while one was open for 4% -> 0% of each run, Pallas kernels for 0% -> 11%
where the time goes in v1:
time: 32.2 us; the launch traced here: 32 us
  starting transfers between devices  11.4 us (35%)
  blocking collectives  9.91 us (31%)
  Pallas kernels  5.11 us (16%)
  waiting for transfers between devices  4.86 us (15%)
  between operations  0.68 us (2%)
    all_to_all x1, blocking collectives, on_device(): lax.all_to_all(message, 'dp', split_axis=0, concat_axis=0, tiled=True)  9.91 us
    ppermute x4, starting transfers between devices, fetch(): lax.ppermute(block, axis, [(shifted(i, stride, radix, by), i) for i in ra...  7.66 us
    pallas_call x5, Pallas kernels, call(): pl.pallas_call(kernel, out_shape=out_shape, in_specs=[pl.BlockSpec(memory...  5.11 us
    ppermute x3, waiting for transfers between devices, on_device(): lax.ppermute(message, 'mp', [(moved(i, offset, mp_digits), i) for i in ra...  3.45 us
    ppermute x3, starting transfers between devices, on_device(): lax.ppermute(message, 'mp', [(moved(i, offset, mp_digits), i) for i in ra...  1.92 us
    ppermute x3, starting transfers between devices, on_device(): lax.ppermute(patches, 'mp', [(moved(i, offset, mp_digits), i) for i in ra...  1.86 us
    ppermute x4, waiting for transfers between devices, fetch(): lax.ppermute(block, axis, [(shifted(i, stride, radix, by), i) for i in ra...  1.4 us
  transfers between devices with their start and end apart: 10, of which 4 were waited for; matrix products, arithmetic and copies ran while one was open for 0% of the time, Pallas kernels for 11%

profile of v1, /device:TPU:0, one launch (start us, length us, event | category | flops | bytes accessed | tf_op | source)
XLA Modules:
  0.0 32.0 jit_solution(13669169381832125977)
XLA Ops:
  0.6 4.1 %collective-permute-start.3 = (bf16[2,1152]{1,0:T(2,128)(2,1)}, bf16[2,1152]{1,0:T(2,128)(2,1)S(1)}, u32[]{:S(2)}, u32[]{:S(2)}) collective-permute-start(bf16[2,1152]{1,0:T(2,128)(2,1)} %refs_5_.1), channel_id=1, source_target_pairs={{16,0},{20,4},{24,8},{28,12},{0,16},{4,20},{8,24},{12,28},{17,1},{... | collective-permute-start | bytes 13832 | tf_op jit(solution)/shard_map/ppermute | solution.py:54
  4.7 0.0 collective-permute-start
  4.7 1.5 %collective-permute-start.1 = (bf16[288,128]{1,0:T(8,128)(2,1)}, bf16[288,128]{1,0:T(8,128)(2,1)S(1)}, u32[]{:S(2)}, u32[]{:S(2)}) collective-permute-start(bf16[288,128]{1,0:T(8,128)(2,1)} %refs_2_.1), channel_id=1, source_target_pairs={{2,0},{3,1},{0,2},{1,3},{6,4},{7,5},{4,6},{5,7},{10,8},{11,9},{8,1... | collective-permute-start | bytes 221192 | tf_op jit(solution)/shard_map/ppermute | solution.py:266
  6.2 0.4 %collective-permute-start.2 = (bf16[288,128]{1,0:T(8,128)(2,1)}, bf16[288,128]{1,0:T(8,128)(2,1)S(1)}, u32[]{:S(2)}, u32[]{:S(2)}) collective-permute-start(bf16[288,128]{1,0:T(8,128)(2,1)} %refs_2_.1), channel_id=1, source_target_pairs={{3,0},{2,1},{1,2},{0,3},{7,4},{6,5},{5,6},{4,7},{11,8},{10,9},{9,1... | collective-permute-start | bytes 221192 | tf_op jit(solution)/shard_map/ppermute | solution.py:266
  6.6 1.8 %shard_map.77 = (bf16[288,128]{1,0:T(8,128)(2,1)S(1)}, bf16[3,288,1152]{2,1,0:T(8,128)(2,1)S(1)}, bf16[288,1152]{1,0:T(8,128)(2,1)S(1)}, bf16[2,1152]{1,0:T(2,12...) custom-call(s32[64]{0:T(128)} %refs_0_.1, ...), custom_call_target="tpu_custom_call" | custom-call | bytes 5971968 | tf_op jit(solution)/shard_map/pallas_call | solution.py:221
  8.4 0.0 collective-permute-done.3
  8.4 2.6 %collective-permute-start.4 = (bf16[4,1152]{1,0:T(4,128)(2,1)S(1)}, bf16[4,1152]{1,0:T(4,128)(2,1)S(1)}, u32[]{:S(2)}, u32[]{:S(2)}) collective-permute-start(bf16[4,1152]{1,0:T(4,128)(2,1)S(1)} %pad_maximum_fusion.refs_0_), channel_id=1, source_target_pairs={{12,0},{8,4},{4,8},{0,12},{28,16},{24,20},{20,24},{16,28},{13,1},{... | collective-permute-start | bytes 27656 | tf_op jit(solution)/shard_map/ppermute | solution.py:54
  11.0 0.4 %collective-permute-start.5 = (bf16[4,1152]{1,0:T(4,128)(2,1)S(1)}, bf16[4,1152]{1,0:T(4,128)(2,1)S(1)}, u32[]{:S(2)}, u32[]{:S(2)}) collective-permute-start(bf16[4,1152]{1,0:T(4,128)(2,1)S(1)} %pad_maximum_fusion.refs_0_), channel_id=1, source_target_pairs={{8,0},{12,4},{0,8},{4,12},{24,16},{28,20},{16,24},{20,28},{9,1},{1... | collective-permute-start | bytes 27656 | tf_op jit(solution)/shard_map/ppermute | solution.py:54
  11.5 0.0 collective-permute-done.refs_1_
  11.5 0.5 %collective-permute-start.6 = (bf16[4,1152]{1,0:T(4,128)(2,1)S(1)}, bf16[4,1152]{1,0:T(4,128)(2,1)S(1)}, u32[]{:S(2)}, u32[]{:S(2)}) collective-permute-start(bf16[4,1152]{1,0:T(4,128)(2,1)S(1)} %pad_maximum_fusion.refs_0_), channel_id=1, source_target_pairs={{4,0},{0,4},{12,8},{8,12},{20,16},{16,20},{28,24},{24,28},{5,1},{1... | collective-permute-start | bytes 27656 | tf_op jit(solution)/shard_map/ppermute | solution.py:54
  12.0 0.0 collective-permute-done.1.refs_2_
  12.0 0.0 collective-permute-done.2.refs_3_
  12.0 1.7 %shard_map.78 = (f32[8,1152]{1,0:T(8,128)S(1)}, f32[8,1152]{1,0:T(8,128)S(1)}) custom-call(bf16[288,128]{1,0:T(8,128)(2,1)S(1)} %get-tuple-element.13.refs_0_, bf16[288,128]{1,0:T(8,128)(2,1)S(1)} %collective-permute-done.refs_1_, bf16[288,128]{1,0:T(8,128)(2,1)S(1)} %collective-permute-done.1.refs_2_, bf16[288,128]{1,0:T(8,128)(2,1)S(1)} %collective-permute-done.2.refs_3_, ...), custom_call_target="tpu_custom_call" | custom-call | tf_op jit(solution)/shard_map/pallas_call | solution.py:221
  13.7 0.0 collective-permute-done.4.refs_1_
  13.7 0.9 %collective-permute-done.5.refs_2_ = bf16[4,1152]{1,0:T(4,128)(2,1)S(1)} collective-permute-done((bf16[4,1152]{1,0:T(4,128)(2,1)S(1)}, bf16[4,1152]{1,0:T(4,128)(2,1)S(1)}, u32[]{:S(2)}, u32[]{:S(2)}) %collective-permute-start.5) | collective-permute-done | bytes 9248 | tf_op jit(solution)/shard_map/ppermute | solution.py:54
  14.7 0.5 %collective-permute-done.6.refs_3_ = bf16[4,1152]{1,0:T(4,128)(2,1)S(1)} collective-permute-done((bf16[4,1152]{1,0:T(4,128)(2,1)S(1)}, bf16[4,1152]{1,0:T(4,128)(2,1)S(1)}, u32[]{:S(2)}, u32[]{:S(2)}) %collective-permute-start.6) | collective-permute-done | bytes 9248 | tf_op jit(solution)/shard_map/ppermute | solution.py:54
  15.1 0.1 shard_map.79.refs_3_
  15.2 0.1 collective-permute-start.7
  15.3 1.6 %collective-permute-start.8 = (bf16[24,1152]{1,0:T(8,128)(2,1)S(1)}, bf16[24,1152]{1,0:T(8,128)(2,1)S(1)}, u32[]{:S(2)}, u32[]{:S(2)}) collective-permute-start(bf16[24,1152]{1,0:T(8,128)(2,1)S(1)} %shard_map.79.refs_3_), channel_id=1, source_target_pairs={{2,0},{3,1},{0,2},{1,3},{6,4},{7,5},{4,6},{5,7},{10,8},{11,9},{8,1... | collective-permute-start | bytes 165896 | tf_op jit(solution)/shard_map/ppermute | solution.py:284
  16.9 0.3 collective-permute-start.9
  17.2 2.3 %collective-permute-done.7.refs_4_ = bf16[24,1152]{1,0:T(8,128)(2,1)S(1)} collective-permute-done((bf16[24,1152]{1,0:T(8,128)(2,1)S(1)}, bf16[24,1152]{1,0:T(8,128)(2,1)S(1)}, u32[]{:S(2)}, u32[]{:S(2)}) %collective-permute-start.7) | collective-permute-done | bytes 55328 | tf_op jit(solution)/shard_map/ppermute | solution.py:284
  19.4 1.2 %collective-permute-done.8.refs_5_ = bf16[24,1152]{1,0:T(8,128)(2,1)S(1)} collective-permute-done((bf16[24,1152]{1,0:T(8,128)(2,1)S(1)}, bf16[24,1152]{1,0:T(8,128)(2,1)S(1)}, u32[]{:S(2)}, u32[]{:S(2)}) %collective-permute-start.8) | collective-permute-done | bytes 55328 | tf_op jit(solution)/shard_map/ppermute | solution.py:284
  20.6 0.0 collective-permute-done.9.refs_6_
  20.6 0.8 %shard_map.80 = bf16[8,2,1296]{2,1,0:T(2,128)(2,1)S(1)} custom-call(f32[8,8]{1,0:T(8,128)S(1)} %get-tuple-element.12.refs_0_, f32[8,1152]{1,0:T(8,128)S(1)} %get-tuple-element.19.refs_1_, f32[8,1152]{1,0:T(8,128)S(1)} %get-tuple-element.20.refs_4_.refs_2_, bf16[24,1152]{1,0:T(8,128)(2,1)S(1)} %shard_map.79.refs_3_, ...), custom_call_target="tpu_custom_call" | custom-call | tf_op jit(solution)/shard_map/pallas_call | solution.py:221
  21.4 9.9 %all_to_all.5.message = bf16[8,2,1296]{2,1,0:T(2,128)(2,1)S(1)} all-to-all(bf16[8,2,1296]{2,1,0:T(2,128)(2,1)S(1)} %shard_map.80), channel_id=1, replica_groups=mesh['dp'=8,'mp'=4] {'dp'}, dimensions={0} | all-to-all | bytes 82944 | tf_op jit(solution)/shard_map/all_to_all | solution.py:292
  31.3 0.7 %shard_map.81 = (f32[8,288]{1,0:T(8,128)}, f32[2,1152]{1,0:T(2,128)}) custom-call(bf16[8,2,1296]{2,1,0:T(2,128)(2,1)S(1)} %all_to_all.5.message), custom_call_target="tpu_custom_call" | custom-call | tf_op jit(solution)/shard_map/pallas_call | solution.py:221
  (1 shorter events, 0.0 us)
Async XLA Ops:
  0.6 7.8 %collective-permute-start.3 = (bf16[2,1152]{1,0:T(2,128)(2,1)}, bf16[2,1152]{1,0:T(2,128)(2,1)S(1)}, u32[]{:S(2)}, u32[]{:S(2)}) collective-permute-start(bf16[2,1152]{1,0:T(2,128)(2,1)} %refs_5_.1), channel_id=1, source_target_pairs={{16,0},{20,4},{24,8},{28,12},{0,16},{4,20},{8,24},{12,28},{17,1},{... | collective-permute-start | bytes 13832 | tf_op jit(solution)/shard_map/ppermute | solution.py:54
  4.7 6.7 %collective-permute-start = (bf16[288,128]{1,0:T(8,128)(2,1)}, bf16[288,128]{1,0:T(8,128)(2,1)S(1)}, u32[]{:S(2)}, u32[]{:S(2)}) collective-permute-start(bf16[288,128]{1,0:T(8,128)(2,1)} %refs_2_.1), channel_id=1, source_target_pairs={{1,0},{0,1},{3,2},{2,3},{5,4},{4,5},{7,6},{6,7},{9,8},{8,9},{11,10... | collective-permute-start | bytes 221192 | tf_op jit(solution)/shard_map/ppermute | solution.py:266
  4.7 7.2 %collective-permute-start.1 = (bf16[288,128]{1,0:T(8,128)(2,1)}, bf16[288,128]{1,0:T(8,128)(2,1)S(1)}, u32[]{:S(2)}, u32[]{:S(2)}) collective-permute-start(bf16[288,128]{1,0:T(8,128)(2,1)} %refs_2_.1), channel_id=1, source_target_pairs={{2,0},{3,1},{0,2},{1,3},{6,4},{7,5},{4,6},{5,7},{10,8},{11,9},{8,1... | collective-permute-start | bytes 221192 | tf_op jit(solution)/shard_map/ppermute | solution.py:266
  6.2 5.8 %collective-permute-start.2 = (bf16[288,128]{1,0:T(8,128)(2,1)}, bf16[288,128]{1,0:T(8,128)(2,1)S(1)}, u32[]{:S(2)}, u32[]{:S(2)}) collective-permute-start(bf16[288,128]{1,0:T(8,128)(2,1)} %refs_2_.1), channel_id=1, source_target_pairs={{3,0},{2,1},{1,2},{0,3},{7,4},{6,5},{5,6},{4,7},{11,8},{10,9},{9,1... | collective-permute-start | bytes 221192 | tf_op jit(solution)/shard_map/ppermute | solution.py:266
  8.4 5.3 %collective-permute-start.4 = (bf16[4,1152]{1,0:T(4,128)(2,1)S(1)}, bf16[4,1152]{1,0:T(4,128)(2,1)S(1)}, u32[]{:S(2)}, u32[]{:S(2)}) collective-permute-start(bf16[4,1152]{1,0:T(4,128)(2,1)S(1)} %pad_maximum_fusion.refs_0_), channel_id=1, source_target_pairs={{12,0},{8,4},{4,8},{0,12},{28,16},{24,20},{20,24},{16,28},{13,1},{... | collective-permute-start | bytes 27656 | tf_op jit(solution)/shard_map/ppermute | solution.py:54
  11.0 3.7 %collective-permute-start.5 = (bf16[4,1152]{1,0:T(4,128)(2,1)S(1)}, bf16[4,1152]{1,0:T(4,128)(2,1)S(1)}, u32[]{:S(2)}, u32[]{:S(2)}) collective-permute-start(bf16[4,1152]{1,0:T(4,128)(2,1)S(1)} %pad_maximum_fusion.refs_0_), channel_id=1, source_target_pairs={{8,0},{12,4},{0,8},{4,12},{24,16},{28,20},{16,24},{20,28},{9,1},{1... | collective-permute-start | bytes 27656 | tf_op jit(solution)/shard_map/ppermute | solution.py:54
  11.5 3.7 %collective-permute-start.6 = (bf16[4,1152]{1,0:T(4,128)(2,1)S(1)}, bf16[4,1152]{1,0:T(4,128)(2,1)S(1)}, u32[]{:S(2)}, u32[]{:S(2)}) collective-permute-start(bf16[4,1152]{1,0:T(4,128)(2,1)S(1)} %pad_maximum_fusion.refs_0_), channel_id=1, source_target_pairs={{4,0},{0,4},{12,8},{8,12},{20,16},{16,20},{28,24},{24,28},{5,1},{1... | collective-permute-start | bytes 27656 | tf_op jit(solution)/shard_map/ppermute | solution.py:54
  15.2 4.2 %collective-permute-start.7 = (bf16[24,1152]{1,0:T(8,128)(2,1)S(1)}, bf16[24,1152]{1,0:T(8,128)(2,1)S(1)}, u32[]{:S(2)}, u32[]{:S(2)}) collective-permute-start(bf16[24,1152]{1,0:T(8,128)(2,1)S(1)} %shard_map.79.refs_3_), channel_id=1, source_target_pairs={{3,0},{2,1},{1,2},{0,3},{7,4},{6,5},{5,6},{4,7},{11,8},{10,9},{9,1... | collective-permute-start | bytes 165896 | tf_op jit(solution)/shard_map/ppermute | solution.py:284
  15.3 5.3 %collective-permute-start.8 = (bf16[24,1152]{1,0:T(8,128)(2,1)S(1)}, bf16[24,1152]{1,0:T(8,128)(2,1)S(1)}, u32[]{:S(2)}, u32[]{:S(2)}) collective-permute-start(bf16[24,1152]{1,0:T(8,128)(2,1)S(1)} %shard_map.79.refs_3_), channel_id=1, source_target_pairs={{2,0},{3,1},{0,2},{1,3},{6,4},{7,5},{4,6},{5,7},{10,8},{11,9},{8,1... | collective-permute-start | bytes 165896 | tf_op jit(solution)/shard_map/ppermute | solution.py:284
  16.9 3.7 %collective-permute-start.9 = (bf16[24,1152]{1,0:T(8,128)(2,1)S(1)}, bf16[24,1152]{1,0:T(8,128)(2,1)S(1)}, u32[]{:S(2)}, u32[]{:S(2)}) collective-permute-start(bf16[24,1152]{1,0:T(8,128)(2,1)S(1)} %shard_map.79.refs_3_), channel_id=1, source_target_pairs={{1,0},{0,1},{3,2},{2,3},{5,4},{4,5},{7,6},{6,7},{9,8},{8,9},{11,10... | collective-permute-start | bytes 165896 | tf_op jit(solution)/shard_map/ppermute | solution.py:284

commit v2 on v1

--- a/solution.py
+++ b/solution.py
@@ -124,16 +124,12 @@
     belongs = member[...]
     count = jnp.sum(belongs, axis=1, keepdims=True)
     patch_mean[...] = dot(belongs.astype(BF16), x.astype(BF16), LAST_LAST) / count
-    queries = []
-    for head in range(heads):
-        above, below = head * HD, (heads - 1 - head) * HD
-        own = query[above : above + HD]
-        blocks = [jnp.zeros((above, rows), F32)] * (above > 0) + [own]
-        blocks += [jnp.zeros((below, rows), F32)] * (below > 0)
-        queries.append(jnp.concatenate(blocks, axis=0))
+    row_head = iota(query.shape, 0) // HD
+    queries = [jnp.where(row_head == head, query, 0.0) for head in range(heads)]
     queries = jnp.concatenate(queries, axis=1).astype(BF16)
     scores = dot(key.T.astype(BF16), queries) * (1.0 / math.sqrt(HD))
-    scores = scores + jnp.concatenate([bias[...]] * heads, axis=1)
+    same = jnp.concatenate([bias[...]] * heads, axis=1) > -1.0
+    scores = jnp.where(same, scores, -1e30)
     raised = jnp.exp(scores - jnp.max(scores, axis=0, keepdims=True))
     weights = (raised * (1.0 / jnp.sum(raised, axis=0, keepdims=True))).astype(BF16)
     pooling = dot(spread[...].astype(BF16), weights, LAST_LAST).astype(BF16)
@@ -185,18 +181,16 @@
         logits = 4.0 * logits - 2.0
         return -4.0 * label * jax.nn.sigmoid(-label * logits)
 
+    own_columns = text_unit[:, :slice_width]
+    for lane in range(1, lanes):
+        block = text_unit[:, lane * slice_width : (lane + 1) * slice_width]
+        own_columns = jnp.where(mp_index == lane, block, own_columns)
     by_image = scaled(dot(image_unit, text_unit, LAST_LAST), 0, 1)
-    by_text = scaled(dot(text_unit[:group], image_unit, LAST_LAST), 1, 0).astype(BF16)
-
+    text_grad = dot(by_image[:, :group].astype(BF16), image_unit, FIRST_FIRST)
     goes = chosen[...]
     rows = sum(goes[:, image : image + 1] * by_image[image : image + 1] for image in range(images))
-    image_grad = dot(rows.astype(BF16), text_unit)
-    own_columns = image_grad[:, :slice_width]
-    for lane in range(1, lanes):
-        block = image_grad[:, lane * slice_width : (lane + 1) * slice_width]
-        own_columns = jnp.where(mp_index == lane, block, own_columns)
-    text_grad = dot(by_text, image_unit)
-    parts = [own_columns[:, which * part : (which + 1) * part] for which in range(texts_here)]
+    image_grad = dot(rows.astype(BF16), own_columns)
+    parts = [image_grad[:, which * part : (which + 1) * part] for which in range(texts_here)]
     for position in range(devices):
         first = position * texts_here
         row = [block[position : position + 1] for block in parts]

time: 32.2 us -> 32 us (level)
  no operation moved by 1% of the time
where the time goes in v2:
time: 32 us; the launch traced here: 31.8 us
  starting transfers between devices  11.4 us (36%)
  blocking collectives  9.91 us (31%)
  Pallas kernels  4.88 us (15%)
  waiting for transfers between devices  4.86 us (15%)
  between operations  0.69 us (2%)
    all_to_all x1, blocking collectives, on_device(): lax.all_to_all(message, 'dp', split_axis=0, concat_axis=0, tiled=True)  9.91 us
    ppermute x4, starting transfers between devices, fetch(): lax.ppermute(block, axis, [(shifted(i, stride, radix, by), i) for i in ra...  7.66 us
    pallas_call x5, Pallas kernels, call(): pl.pallas_call(kernel, out_shape=out_shape, in_specs=[pl.BlockSpec(memory...  4.88 us
    ppermute x3, waiting for transfers between devices, on_device(): lax.ppermute(message, 'mp', [(moved(i, offset, mp_digits), i) for i in ra...  3.45 us
    ppermute x3, starting transfers between devices, on_device(): lax.ppermute(message, 'mp', [(moved(i, offset, mp_digits), i) for i in ra...  1.92 us
    ppermute x3, starting transfers between devices, on_device(): lax.ppermute(patches, 'mp', [(moved(i, offset, mp_digits), i) for i in ra...  1.86 us
    ppermute x4, waiting for transfers between devices, fetch(): lax.ppermute(block, axis, [(shifted(i, stride, radix, by), i) for i in ra...  1.4 us
  transfers between devices with their start and end apart: 10, of which 4 were waited for; matrix products, arithmetic and copies ran while one was open for 0% of the time, Pallas kernels for 11%

profile of v2, /device:TPU:0, one launch (start us, length us, event | category | flops | bytes accessed | tf_op | source)
XLA Modules:
  0.0 31.8 jit_solution(9160858680269468331)
XLA Ops:
  0.6 4.1 %collective-permute-start.3 = (bf16[2,1152]{1,0:T(2,128)(2,1)}, bf16[2,1152]{1,0:T(2,128)(2,1)S(1)}, u32[]{:S(2)}, u32[]{:S(2)}) collective-permute-start(bf16[2,1152]{1,0:T(2,128)(2,1)} %refs_5_.1), channel_id=1, source_target_pairs={{16,0},{20,4},{24,8},{28,12},{0,16},{4,20},{8,24},{12,28},{17,1},{... | collective-permute-start | bytes 13832 | tf_op jit(solution)/shard_map/ppermute | solution.py:54
  4.7 0.0 collective-permute-start
  4.7 1.5 %collective-permute-start.1 = (bf16[288,128]{1,0:T(8,128)(2,1)}, bf16[288,128]{1,0:T(8,128)(2,1)S(1)}, u32[]{:S(2)}, u32[]{:S(2)}) collective-permute-start(bf16[288,128]{1,0:T(8,128)(2,1)} %refs_2_.1), channel_id=1, source_target_pairs={{2,0},{3,1},{0,2},{1,3},{6,4},{7,5},{4,6},{5,7},{10,8},{11,9},{8,1... | collective-permute-start | bytes 221192 | tf_op jit(solution)/shard_map/ppermute | solution.py:260
  6.2 0.4 %collective-permute-start.2 = (bf16[288,128]{1,0:T(8,128)(2,1)}, bf16[288,128]{1,0:T(8,128)(2,1)S(1)}, u32[]{:S(2)}, u32[]{:S(2)}) collective-permute-start(bf16[288,128]{1,0:T(8,128)(2,1)} %refs_2_.1), channel_id=1, source_target_pairs={{3,0},{2,1},{1,2},{0,3},{7,4},{6,5},{5,6},{4,7},{11,8},{10,9},{9,1... | collective-permute-start | bytes 221192 | tf_op jit(solution)/shard_map/ppermute | solution.py:260
  6.6 1.8 %shard_map.77 = (bf16[288,128]{1,0:T(8,128)(2,1)S(1)}, bf16[3,288,1152]{2,1,0:T(8,128)(2,1)S(1)}, bf16[288,1152]{1,0:T(8,128)(2,1)S(1)}, bf16[2,1152]{1,0:T(2,12...) custom-call(s32[64]{0:T(128)} %refs_0_.1, ...), custom_call_target="tpu_custom_call" | custom-call | bytes 5971968 | tf_op jit(solution)/shard_map/pallas_call | solution.py:215
  8.4 0.0 collective-permute-done.3
  8.4 2.6 %collective-permute-start.4 = (bf16[4,1152]{1,0:T(4,128)(2,1)S(1)}, bf16[4,1152]{1,0:T(4,128)(2,1)S(1)}, u32[]{:S(2)}, u32[]{:S(2)}) collective-permute-start(bf16[4,1152]{1,0:T(4,128)(2,1)S(1)} %pad_maximum_fusion.refs_0_), channel_id=1, source_target_pairs={{12,0},{8,4},{4,8},{0,12},{28,16},{24,20},{20,24},{16,28},{13,1},{... | collective-permute-start | bytes 27656 | tf_op jit(solution)/shard_map/ppermute | solution.py:54
  11.0 0.4 %collective-permute-start.5 = (bf16[4,1152]{1,0:T(4,128)(2,1)S(1)}, bf16[4,1152]{1,0:T(4,128)(2,1)S(1)}, u32[]{:S(2)}, u32[]{:S(2)}) collective-permute-start(bf16[4,1152]{1,0:T(4,128)(2,1)S(1)} %pad_maximum_fusion.refs_0_), channel_id=1, source_target_pairs={{8,0},{12,4},{0,8},{4,12},{24,16},{28,20},{16,24},{20,28},{9,1},{1... | collective-permute-start | bytes 27656 | tf_op jit(solution)/shard_map/ppermute | solution.py:54
  11.5 0.0 collective-permute-done.refs_1_
  11.5 0.5 %collective-permute-start.6 = (bf16[4,1152]{1,0:T(4,128)(2,1)S(1)}, bf16[4,1152]{1,0:T(4,128)(2,1)S(1)}, u32[]{:S(2)}, u32[]{:S(2)}) collective-permute-start(bf16[4,1152]{1,0:T(4,128)(2,1)S(1)} %pad_maximum_fusion.refs_0_), channel_id=1, source_target_pairs={{4,0},{0,4},{12,8},{8,12},{20,16},{16,20},{28,24},{24,28},{5,1},{1... | collective-permute-start | bytes 27656 | tf_op jit(solution)/shard_map/ppermute | solution.py:54
  12.0 0.0 collective-permute-done.1.refs_2_
  12.0 0.0 collective-permute-done.2.refs_3_
  12.0 1.7 %shard_map.78 = (f32[8,1152]{1,0:T(8,128)S(1)}, f32[8,1152]{1,0:T(8,128)S(1)}) custom-call(bf16[288,128]{1,0:T(8,128)(2,1)S(1)} %get-tuple-element.13.refs_0_, bf16[288,128]{1,0:T(8,128)(2,1)S(1)} %collective-permute-done.refs_1_, bf16[288,128]{1,0:T(8,128)(2,1)S(1)} %collective-permute-done.1.refs_2_, bf16[288,128]{1,0:T(8,128)(2,1)S(1)} %collective-permute-done.2.refs_3_, ...), custom_call_target="tpu_custom_call" | custom-call | tf_op jit(solution)/shard_map/pallas_call | solution.py:215
  13.7 0.0 collective-permute-done.4.refs_1_
  13.7 0.9 %collective-permute-done.5.refs_2_ = bf16[4,1152]{1,0:T(4,128)(2,1)S(1)} collective-permute-done((bf16[4,1152]{1,0:T(4,128)(2,1)S(1)}, bf16[4,1152]{1,0:T(4,128)(2,1)S(1)}, u32[]{:S(2)}, u32[]{:S(2)}) %collective-permute-start.5) | collective-permute-done | bytes 9248 | tf_op jit(solution)/shard_map/ppermute | solution.py:54
  14.7 0.5 %collective-permute-done.6.refs_3_ = bf16[4,1152]{1,0:T(4,128)(2,1)S(1)} collective-permute-done((bf16[4,1152]{1,0:T(4,128)(2,1)S(1)}, bf16[4,1152]{1,0:T(4,128)(2,1)S(1)}, u32[]{:S(2)}, u32[]{:S(2)}) %collective-permute-start.6) | collective-permute-done | bytes 9248 | tf_op jit(solution)/shard_map/ppermute | solution.py:54
  15.1 0.1 shard_map.79.refs_3_
  15.2 0.1 collective-permute-start.7
  15.3 1.6 %collective-permute-start.8 = (bf16[24,1152]{1,0:T(8,128)(2,1)S(1)}, bf16[24,1152]{1,0:T(8,128)(2,1)S(1)}, u32[]{:S(2)}, u32[]{:S(2)}) collective-permute-start(bf16[24,1152]{1,0:T(8,128)(2,1)S(1)} %shard_map.79.refs_3_), channel_id=1, source_target_pairs={{2,0},{3,1},{0,2},{1,3},{6,4},{7,5},{4,6},{5,7},{10,8},{11,9},{8,1... | collective-permute-start | bytes 165896 | tf_op jit(solution)/shard_map/ppermute | solution.py:278
  16.9 0.3 collective-permute-start.9
  17.2 2.3 %collective-permute-done.7.refs_4_ = bf16[24,1152]{1,0:T(8,128)(2,1)S(1)} collective-permute-done((bf16[24,1152]{1,0:T(8,128)(2,1)S(1)}, bf16[24,1152]{1,0:T(8,128)(2,1)S(1)}, u32[]{:S(2)}, u32[]{:S(2)}) %collective-permute-start.7) | collective-permute-done | bytes 55328 | tf_op jit(solution)/shard_map/ppermute | solution.py:278
  19.4 1.2 %collective-permute-done.8.refs_5_ = bf16[24,1152]{1,0:T(8,128)(2,1)S(1)} collective-permute-done((bf16[24,1152]{1,0:T(8,128)(2,1)S(1)}, bf16[24,1152]{1,0:T(8,128)(2,1)S(1)}, u32[]{:S(2)}, u32[]{:S(2)}) %collective-permute-start.8) | collective-permute-done | bytes 55328 | tf_op jit(solution)/shard_map/ppermute | solution.py:278
  20.6 0.0 collective-permute-done.9.refs_6_
  20.6 0.6 %shard_map.80 = bf16[8,2,1296]{2,1,0:T(2,128)(2,1)S(1)} custom-call(f32[8,8]{1,0:T(8,128)S(1)} %get-tuple-element.12.refs_0_, f32[8,1152]{1,0:T(8,128)S(1)} %get-tuple-element.19.refs_1_, f32[8,1152]{1,0:T(8,128)S(1)} %get-tuple-element.20.refs_4_.refs_2_, bf16[24,1152]{1,0:T(8,128)(2,1)S(1)} %shard_map.79.refs_3_, ...), custom_call_target="tpu_custom_call" | custom-call | tf_op jit(solution)/shard_map/pallas_call | solution.py:215
  21.2 9.9 %all_to_all.5.message = bf16[8,2,1296]{2,1,0:T(2,128)(2,1)S(1)} all-to-all(bf16[8,2,1296]{2,1,0:T(2,128)(2,1)S(1)} %shard_map.80), channel_id=1, replica_groups=mesh['dp'=8,'mp'=4] {'dp'}, dimensions={0} | all-to-all | bytes 82944 | tf_op jit(solution)/shard_map/all_to_all | solution.py:286
  31.1 0.7 %shard_map.81 = (f32[8,288]{1,0:T(8,128)}, f32[2,1152]{1,0:T(2,128)}) custom-call(bf16[8,2,1296]{2,1,0:T(2,128)(2,1)S(1)} %all_to_all.5.message), custom_call_target="tpu_custom_call" | custom-call | tf_op jit(solution)/shard_map/pallas_call | solution.py:215
  (1 shorter events, 0.0 us)
Async XLA Ops:
  0.6 7.8 %collective-permute-start.3 = (bf16[2,1152]{1,0:T(2,128)(2,1)}, bf16[2,1152]{1,0:T(2,128)(2,1)S(1)}, u32[]{:S(2)}, u32[]{:S(2)}) collective-permute-start(bf16[2,1152]{1,0:T(2,128)(2,1)} %refs_5_.1), channel_id=1, source_target_pairs={{16,0},{20,4},{24,8},{28,12},{0,16},{4,20},{8,24},{12,28},{17,1},{... | collective-permute-start | bytes 13832 | tf_op jit(solution)/shard_map/ppermute | solution.py:54
  4.7 6.7 %collective-permute-start = (bf16[288,128]{1,0:T(8,128)(2,1)}, bf16[288,128]{1,0:T(8,128)(2,1)S(1)}, u32[]{:S(2)}, u32[]{:S(2)}) collective-permute-start(bf16[288,128]{1,0:T(8,128)(2,1)} %refs_2_.1), channel_id=1, source_target_pairs={{1,0},{0,1},{3,2},{2,3},{5,4},{4,5},{7,6},{6,7},{9,8},{8,9},{11,10... | collective-permute-start | bytes 221192 | tf_op jit(solution)/shard_map/ppermute | solution.py:260
  4.7 7.2 %collective-permute-start.1 = (bf16[288,128]{1,0:T(8,128)(2,1)}, bf16[288,128]{1,0:T(8,128)(2,1)S(1)}, u32[]{:S(2)}, u32[]{:S(2)}) collective-permute-start(bf16[288,128]{1,0:T(8,128)(2,1)} %refs_2_.1), channel_id=1, source_target_pairs={{2,0},{3,1},{0,2},{1,3},{6,4},{7,5},{4,6},{5,7},{10,8},{11,9},{8,1... | collective-permute-start | bytes 221192 | tf_op jit(solution)/shard_map/ppermute | solution.py:260
  6.2 5.8 %collective-permute-start.2 = (bf16[288,128]{1,0:T(8,128)(2,1)}, bf16[288,128]{1,0:T(8,128)(2,1)S(1)}, u32[]{:S(2)}, u32[]{:S(2)}) collective-permute-start(bf16[288,128]{1,0:T(8,128)(2,1)} %refs_2_.1), channel_id=1, source_target_pairs={{3,0},{2,1},{1,2},{0,3},{7,4},{6,5},{5,6},{4,7},{11,8},{10,9},{9,1... | collective-permute-start | bytes 221192 | tf_op jit(solution)/shard_map/ppermute | solution.py:260
  8.4 5.3 %collective-permute-start.4 = (bf16[4,1152]{1,0:T(4,128)(2,1)S(1)}, bf16[4,1152]{1,0:T(4,128)(2,1)S(1)}, u32[]{:S(2)}, u32[]{:S(2)}) collective-permute-start(bf16[4,1152]{1,0:T(4,128)(2,1)S(1)} %pad_maximum_fusion.refs_0_), channel_id=1, source_target_pairs={{12,0},{8,4},{4,8},{0,12},{28,16},{24,20},{20,24},{16,28},{13,1},{... | collective-permute-start | bytes 27656 | tf_op jit(solution)/shard_map/ppermute | solution.py:54
  11.0 3.7 %collective-permute-start.5 = (bf16[4,1152]{1,0:T(4,128)(2,1)S(1)}, bf16[4,1152]{1,0:T(4,128)(2,1)S(1)}, u32[]{:S(2)}, u32[]{:S(2)}) collective-permute-start(bf16[4,1152]{1,0:T(4,128)(2,1)S(1)} %pad_maximum_fusion.refs_0_), channel_id=1, source_target_pairs={{8,0},{12,4},{0,8},{4,12},{24,16},{28,20},{16,24},{20,28},{9,1},{1... | collective-permute-start | bytes 27656 | tf_op jit(solution)/shard_map/ppermute | solution.py:54
  11.5 3.7 %collective-permute-start.6 = (bf16[4,1152]{1,0:T(4,128)(2,1)S(1)}, bf16[4,1152]{1,0:T(4,128)(2,1)S(1)}, u32[]{:S(2)}, u32[]{:S(2)}) collective-permute-start(bf16[4,1152]{1,0:T(4,128)(2,1)S(1)} %pad_maximum_fusion.refs_0_), channel_id=1, source_target_pairs={{4,0},{0,4},{12,8},{8,12},{20,16},{16,20},{28,24},{24,28},{5,1},{1... | collective-permute-start | bytes 27656 | tf_op jit(solution)/shard_map/ppermute | solution.py:54
  15.2 4.2 %collective-permute-start.7 = (bf16[24,1152]{1,0:T(8,128)(2,1)S(1)}, bf16[24,1152]{1,0:T(8,128)(2,1)S(1)}, u32[]{:S(2)}, u32[]{:S(2)}) collective-permute-start(bf16[24,1152]{1,0:T(8,128)(2,1)S(1)} %shard_map.79.refs_3_), channel_id=1, source_target_pairs={{3,0},{2,1},{1,2},{0,3},{7,4},{6,5},{5,6},{4,7},{11,8},{10,9},{9,1... | collective-permute-start | bytes 165896 | tf_op jit(solution)/shard_map/ppermute | solution.py:278
  15.3 5.3 %collective-permute-start.8 = (bf16[24,1152]{1,0:T(8,128)(2,1)S(1)}, bf16[24,1152]{1,0:T(8,128)(2,1)S(1)}, u32[]{:S(2)}, u32[]{:S(2)}) collective-permute-start(bf16[24,1152]{1,0:T(8,128)(2,1)S(1)} %shard_map.79.refs_3_), channel_id=1, source_target_pairs={{2,0},{3,1},{0,2},{1,3},{6,4},{7,5},{4,6},{5,7},{10,8},{11,9},{8,1... | collective-permute-start | bytes 165896 | tf_op jit(solution)/shard_map/ppermute | solution.py:278
  16.9 3.7 %collective-permute-start.9 = (bf16[24,1152]{1,0:T(8,128)(2,1)S(1)}, bf16[24,1152]{1,0:T(8,128)(2,1)S(1)}, u32[]{:S(2)}, u32[]{:S(2)}) collective-permute-start(bf16[24,1152]{1,0:T(8,128)(2,1)S(1)} %shard_map.79.refs_3_), channel_id=1, source_target_pairs={{1,0},{0,1},{3,2},{2,3},{5,4},{4,5},{7,6},{6,7},{9,8},{8,9},{11,10... | collective-permute-start | bytes 165896 | tf_op jit(solution)/shard_map/ppermute | solution.py:278

commit v3 on v2

--- a/solution.py
+++ b/solution.py
@@ -104,7 +104,7 @@
 
 def attend(offsets, *refs):
     lanes = len(offsets)
-    *pieces, bias, member, spread, w_qkv, w_out, share, patch_mean, x_rows = refs
+    *pieces, bias, member, spread, w_qkv, w_out, share, patch_rows, x_rows = refs
     mp_index = lax.axis_index("mp")
     piece_width = pieces[0].shape[0]
     width, rows = x_rows.shape
@@ -123,7 +123,7 @@
 
     belongs = member[...]
     count = jnp.sum(belongs, axis=1, keepdims=True)
-    patch_mean[...] = dot(belongs.astype(BF16), x.astype(BF16), LAST_LAST) / count
+    patch_rows[...] = x.astype(BF16)
     row_head = iota(query.shape, 0) // HD
     queries = [jnp.where(row_head == head, query, 0.0) for head in range(heads)]
     queries = jnp.concatenate(queries, axis=1).astype(BF16)
@@ -141,6 +141,12 @@
         pooled_heads = jnp.where(column_head == head, block, pooled_heads)
     pooled_heads = (pooled_heads / count).astype(BF16)
     share[...] = dot(pooled_heads, w_out[...])
+
+
+def average(member, patch_rows, patch_mean):
+    belongs = member[...]
+    count = jnp.sum(belongs, axis=1, keepdims=True)
+    patch_mean[...] = dot(belongs.astype(BF16), patch_rows[...], LAST_LAST) / count
 
 
 def join(*refs):
@@ -266,11 +272,17 @@
         sent = block if len(texts) > 1 else text
         texts = [block] + [fetch(sent, "dp", stride, radix, by) for by in range(1, radix)]
 
-    share, patch_mean = call(
+    share, patch_rows = call(
         functools.partial(attend, offsets),
-        (shape((images, width), F32), shape((images, width), F32)),
+        (shape((images, width), F32), shape((width, rows), BF16)),
         [patches_here, *pieces, bias, member, spread, w_qkv_here, w_out_here],
         scratch=[pltpu.VMEM((width, rows), F32)],
+    )
+    patch_mean = call(
+        average,
+        shape((images, width), F32),
+        [member, patch_rows],
+        cost=pl.CostEstimate(flops=10**9, bytes_accessed=0, transcendentals=0),
     )
     texts = [texts[0], *texts[:0:-1]]
     message = call(join, shape((devices * texts_here + images, width), BF16), [*texts, share])

time: 32 us -> 32 us (level)
    pallas_call x5 -> x6, Pallas kernels: 4.88 us -> 5.03 us  [call(): pl.pallas_call(kernel, out_shape=out_shape, in_specs=[pl.BlockSpec(memory...]
  transfers between devices with their start and end apart: 10 -> 10, of which waited for: 4 -> 4; matrix products, arithmetic and copies ran while one was open for 0% -> 0% of each run, Pallas kernels for 11% -> 12%
where the time goes in v3:
time: 32 us; the launch traced here: 31.8 us
  starting transfers between devices  11.4 us (36%)
  blocking collectives  9.91 us (31%)
  Pallas kernels  5.03 us (16%)
  waiting for transfers between devices  4.71 us (15%)
  between operations  0.69 us (2%)
    all_to_all x1, blocking collectives, on_device(): lax.all_to_all(message, 'dp', split_axis=0, concat_axis=0, tiled=True)  9.91 us
    ppermute x4, starting transfers between devices, fetch(): lax.ppermute(block, axis, [(shifted(i, stride, radix, by), i) for i in ra...  7.66 us
    pallas_call x6, Pallas kernels, call(): pl.pallas_call(kernel, out_shape=out_shape, in_specs=[pl.BlockSpec(memory...  5.03 us
    ppermute x3, waiting for transfers between devices, on_device(): lax.ppermute(message, 'mp', [(moved(i, offset, mp_digits), i) for i in ra...  3.26 us
    ppermute x3, starting transfers between devices, on_device(): lax.ppermute(message, 'mp', [(moved(i, offset, mp_digits), i) for i in ra...  1.92 us
    ppermute x3, starting transfers between devices, on_device(): lax.ppermute(patches, 'mp', [(moved(i, offset, mp_digits), i) for i in ra...  1.86 us
    ppermute x4, waiting for transfers between devices, fetch(): lax.ppermute(block, axis, [(shifted(i, stride, radix, by), i) for i in ra...  1.44 us
  transfers between devices with their start and end apart: 10, of which 4 were waited for; matrix products, arithmetic and copies ran while one was open for 0% of the time, Pallas kernels for 12%

profile of v3, /device:TPU:0, one launch (start us, length us, event | category | flops | bytes accessed | tf_op | source)
XLA Modules:
  0.0 31.8 jit_solution(14308696405263757859)
XLA Ops:
  0.6 4.1 %collective-permute-start.3 = (bf16[2,1152]{1,0:T(2,128)(2,1)}, bf16[2,1152]{1,0:T(2,128)(2,1)S(1)}, u32[]{:S(2)}, u32[]{:S(2)}) collective-permute-start(bf16[2,1152]{1,0:T(2,128)(2,1)} %refs_5_.1), channel_id=1, source_target_pairs={{16,0},{20,4},{24,8},{28,12},{0,16},{4,20},{8,24},{12,28},{17,1},{... | collective-permute-start | bytes 13832 | tf_op jit(solution)/shard_map/ppermute | solution.py:54
  4.7 0.0 collective-permute-start
  4.7 1.5 %collective-permute-start.1 = (bf16[288,128]{1,0:T(8,128)(2,1)}, bf16[288,128]{1,0:T(8,128)(2,1)S(1)}, u32[]{:S(2)}, u32[]{:S(2)}) collective-permute-start(bf16[288,128]{1,0:T(8,128)(2,1)} %refs_2_.1), channel_id=1, source_target_pairs={{2,0},{3,1},{0,2},{1,3},{6,4},{7,5},{4,6},{5,7},{10,8},{11,9},{8,1... | collective-permute-start | bytes 221192 | tf_op jit(solution)/shard_map/ppermute | solution.py:266
  6.2 0.4 %collective-permute-start.2 = (bf16[288,128]{1,0:T(8,128)(2,1)}, bf16[288,128]{1,0:T(8,128)(2,1)S(1)}, u32[]{:S(2)}, u32[]{:S(2)}) collective-permute-start(bf16[288,128]{1,0:T(8,128)(2,1)} %refs_2_.1), channel_id=1, source_target_pairs={{3,0},{2,1},{1,2},{0,3},{7,4},{6,5},{5,6},{4,7},{11,8},{10,9},{9,1... | collective-permute-start | bytes 221192 | tf_op jit(solution)/shard_map/ppermute | solution.py:266
  6.6 1.8 %shard_map.77 = (bf16[288,128]{1,0:T(8,128)(2,1)S(1)}, bf16[3,288,1152]{2,1,0:T(8,128)(2,1)S(1)}, bf16[288,1152]{1,0:T(8,128)(2,1)S(1)}, bf16[2,1152]{1,0:T(2,12...) custom-call(s32[64]{0:T(128)} %refs_0_.1, ...), custom_call_target="tpu_custom_call" | custom-call | bytes 5971968 | tf_op jit(solution)/shard_map/pallas_call | solution.py:221
  8.4 0.0 collective-permute-done.3
  8.4 2.6 %collective-permute-start.4 = (bf16[4,1152]{1,0:T(4,128)(2,1)S(1)}, bf16[4,1152]{1,0:T(4,128)(2,1)S(1)}, u32[]{:S(2)}, u32[]{:S(2)}) collective-permute-start(bf16[4,1152]{1,0:T(4,128)(2,1)S(1)} %pad_maximum_fusion.refs_0_), channel_id=1, source_target_pairs={{12,0},{8,4},{4,8},{0,12},{28,16},{24,20},{20,24},{16,28},{13,1},{... | collective-permute-start | bytes 27656 | tf_op jit(solution)/shard_map/ppermute | solution.py:54
  11.0 0.4 %collective-permute-start.5 = (bf16[4,1152]{1,0:T(4,128)(2,1)S(1)}, bf16[4,1152]{1,0:T(4,128)(2,1)S(1)}, u32[]{:S(2)}, u32[]{:S(2)}) collective-permute-start(bf16[4,1152]{1,0:T(4,128)(2,1)S(1)} %pad_maximum_fusion.refs_0_), channel_id=1, source_target_pairs={{8,0},{12,4},{0,8},{4,12},{24,16},{28,20},{16,24},{20,28},{9,1},{1... | collective-permute-start | bytes 27656 | tf_op jit(solution)/shard_map/ppermute | solution.py:54
  11.5 0.0 collective-permute-done.refs_1_
  11.5 0.5 %collective-permute-start.6 = (bf16[4,1152]{1,0:T(4,128)(2,1)S(1)}, bf16[4,1152]{1,0:T(4,128)(2,1)S(1)}, u32[]{:S(2)}, u32[]{:S(2)}) collective-permute-start(bf16[4,1152]{1,0:T(4,128)(2,1)S(1)} %pad_maximum_fusion.refs_0_), channel_id=1, source_target_pairs={{4,0},{0,4},{12,8},{8,12},{20,16},{16,20},{28,24},{24,28},{5,1},{1... | collective-permute-start | bytes 27656 | tf_op jit(solution)/shard_map/ppermute | solution.py:54
  12.0 0.0 collective-permute-done.1.refs_2_
  12.0 0.0 collective-permute-done.2.refs_3_
  12.0 1.7 %shard_map.78 = (f32[8,1152]{1,0:T(8,128)S(1)}, bf16[1152,128]{1,0:T(8,128)(2,1)S(1)}) custom-call(bf16[288,128]{1,0:T(8,128)(2,1)S(1)} %get-tuple-element.14.refs_0_, bf16[288,128]{1,0:T(8,128)(2,1)S(1)} %collective-permute-done.refs_1_, bf16[288,128]{1,0:T(8,128)(2,1)S(1)} %collective-permute-done.1.refs_2_, ...), custom_call_target="tpu_custom_call" | custom-call | tf_op jit(solution)/shard_map/pallas_call | solution.py:221
  13.7 0.0 collective-permute-done.4.refs_1_
  13.7 1.0 %collective-permute-done.5.refs_2_ = bf16[4,1152]{1,0:T(4,128)(2,1)S(1)} collective-permute-done((bf16[4,1152]{1,0:T(4,128)(2,1)S(1)}, bf16[4,1152]{1,0:T(4,128)(2,1)S(1)}, u32[]{:S(2)}, u32[]{:S(2)}) %collective-permute-start.5) | collective-permute-done | bytes 9248 | tf_op jit(solution)/shard_map/ppermute | solution.py:54
  14.7 0.5 %collective-permute-done.6.refs_3_ = bf16[4,1152]{1,0:T(4,128)(2,1)S(1)} collective-permute-done((bf16[4,1152]{1,0:T(4,128)(2,1)S(1)}, bf16[4,1152]{1,0:T(4,128)(2,1)S(1)}, u32[]{:S(2)}, u32[]{:S(2)}) %collective-permute-start.6) | collective-permute-done | bytes 9248 | tf_op jit(solution)/shard_map/ppermute | solution.py:54
  15.1 0.1 shard_map.80.refs_3_
  15.2 0.1 collective-permute-start.7
  15.3 1.6 %collective-permute-start.8 = (bf16[24,1152]{1,0:T(8,128)(2,1)S(1)}, bf16[24,1152]{1,0:T(8,128)(2,1)S(1)}, u32[]{:S(2)}, u32[]{:S(2)}) collective-permute-start(bf16[24,1152]{1,0:T(8,128)(2,1)S(1)} %shard_map.80.refs_3_), channel_id=1, source_target_pairs={{2,0},{3,1},{0,2},{1,3},{6,4},{7,5},{4,6},{5,7},{10,8},{11,9},{8,1... | collective-permute-start | bytes 165896 | tf_op jit(solution)/shard_map/ppermute | solution.py:290
  16.9 0.3 collective-permute-start.9
  17.2 0.2 shard_map.79.refs_1_
  17.4 2.1 %collective-permute-done.7.refs_4_ = bf16[24,1152]{1,0:T(8,128)(2,1)S(1)} collective-permute-done((bf16[24,1152]{1,0:T(8,128)(2,1)S(1)}, bf16[24,1152]{1,0:T(8,128)(2,1)S(1)}, u32[]{:S(2)}, u32[]{:S(2)}) %collective-permute-start.7) | collective-permute-done | bytes 55328 | tf_op jit(solution)/shard_map/ppermute | solution.py:290
  19.4 1.2 %collective-permute-done.8.refs_5_ = bf16[24,1152]{1,0:T(8,128)(2,1)S(1)} collective-permute-done((bf16[24,1152]{1,0:T(8,128)(2,1)S(1)}, bf16[24,1152]{1,0:T(8,128)(2,1)S(1)}, u32[]{:S(2)}, u32[]{:S(2)}) %collective-permute-start.8) | collective-permute-done | bytes 55328 | tf_op jit(solution)/shard_map/ppermute | solution.py:290
  20.6 0.0 collective-permute-done.9.refs_6_
  20.6 0.6 %shard_map.81 = bf16[8,2,1296]{2,1,0:T(2,128)(2,1)S(1)} custom-call(f32[8,8]{1,0:T(8,128)S(1)} %get-tuple-element.12.refs_0_, f32[8,1152]{1,0:T(8,128)S(1)} %shard_map.79.refs_1_, f32[8,1152]{1,0:T(8,128)S(1)} %get-tuple-element.20.refs_4_.refs_2_, bf16[24,1152]{1,0:T(8,128)(2,1)S(1)} %shard_map.80.refs_3_, ...), custom_call_target="tpu_custom_call" | custom-call | tf_op jit(solution)/shard_map/pallas_call | solution.py:221
  21.2 9.9 %all_to_all.5.message = bf16[8,2,1296]{2,1,0:T(2,128)(2,1)S(1)} all-to-all(bf16[8,2,1296]{2,1,0:T(2,128)(2,1)S(1)} %shard_map.81), channel_id=1, replica_groups=mesh['dp'=8,'mp'=4] {'dp'}, dimensions={0} | all-to-all | bytes 82944 | tf_op jit(solution)/shard_map/all_to_all | solution.py:298
  31.1 0.7 %shard_map.82 = (f32[8,288]{1,0:T(8,128)}, f32[2,1152]{1,0:T(2,128)}) custom-call(bf16[8,2,1296]{2,1,0:T(2,128)(2,1)S(1)} %all_to_all.5.message), custom_call_target="tpu_custom_call" | custom-call | tf_op jit(solution)/shard_map/pallas_call | solution.py:221
  (1 shorter events, 0.0 us)
Async XLA Ops:
  0.6 7.8 %collective-permute-start.3 = (bf16[2,1152]{1,0:T(2,128)(2,1)}, bf16[2,1152]{1,0:T(2,128)(2,1)S(1)}, u32[]{:S(2)}, u32[]{:S(2)}) collective-permute-start(bf16[2,1152]{1,0:T(2,128)(2,1)} %refs_5_.1), channel_id=1, source_target_pairs={{16,0},{20,4},{24,8},{28,12},{0,16},{4,20},{8,24},{12,28},{17,1},{... | collective-permute-start | bytes 13832 | tf_op jit(solution)/shard_map/ppermute | solution.py:54
  4.7 6.7 %collective-permute-start = (bf16[288,128]{1,0:T(8,128)(2,1)}, bf16[288,128]{1,0:T(8,128)(2,1)S(1)}, u32[]{:S(2)}, u32[]{:S(2)}) collective-permute-start(bf16[288,128]{1,0:T(8,128)(2,1)} %refs_2_.1), channel_id=1, source_target_pairs={{1,0},{0,1},{3,2},{2,3},{5,4},{4,5},{7,6},{6,7},{9,8},{8,9},{11,10... | collective-permute-start | bytes 221192 | tf_op jit(solution)/shard_map/ppermute | solution.py:266
  4.7 7.2 %collective-permute-start.1 = (bf16[288,128]{1,0:T(8,128)(2,1)}, bf16[288,128]{1,0:T(8,128)(2,1)S(1)}, u32[]{:S(2)}, u32[]{:S(2)}) collective-permute-start(bf16[288,128]{1,0:T(8,128)(2,1)} %refs_2_.1), channel_id=1, source_target_pairs={{2,0},{3,1},{0,2},{1,3},{6,4},{7,5},{4,6},{5,7},{10,8},{11,9},{8,1... | collective-permute-start | bytes 221192 | tf_op jit(solution)/shard_map/ppermute | solution.py:266
  6.2 5.8 %collective-permute-start.2 = (bf16[288,128]{1,0:T(8,128)(2,1)}, bf16[288,128]{1,0:T(8,128)(2,1)S(1)}, u32[]{:S(2)}, u32[]{:S(2)}) collective-permute-start(bf16[288,128]{1,0:T(8,128)(2,1)} %refs_2_.1), channel_id=1, source_target_pairs={{3,0},{2,1},{1,2},{0,3},{7,4},{6,5},{5,6},{4,7},{11,8},{10,9},{9,1... | collective-permute-start | bytes 221192 | tf_op jit(solution)/shard_map/ppermute | solution.py:266
  8.4 5.3 %collective-permute-start.4 = (bf16[4,1152]{1,0:T(4,128)(2,1)S(1)}, bf16[4,1152]{1,0:T(4,128)(2,1)S(1)}, u32[]{:S(2)}, u32[]{:S(2)}) collective-permute-start(bf16[4,1152]{1,0:T(4,128)(2,1)S(1)} %pad_maximum_fusion.refs_0_), channel_id=1, source_target_pairs={{12,0},{8,4},{4,8},{0,12},{28,16},{24,20},{20,24},{16,28},{13,1},{... | collective-permute-start | bytes 27656 | tf_op jit(solution)/shard_map/ppermute | solution.py:54
  11.0 3.7 %collective-permute-start.5 = (bf16[4,1152]{1,0:T(4,128)(2,1)S(1)}, bf16[4,1152]{1,0:T(4,128)(2,1)S(1)}, u32[]{:S(2)}, u32[]{:S(2)}) collective-permute-start(bf16[4,1152]{1,0:T(4,128)(2,1)S(1)} %pad_maximum_fusion.refs_0_), channel_id=1, source_target_pairs={{8,0},{12,4},{0,8},{4,12},{24,16},{28,20},{16,24},{20,28},{9,1},{1... | collective-permute-start | bytes 27656 | tf_op jit(solution)/shard_map/ppermute | solution.py:54
  11.5 3.7 %collective-permute-start.6 = (bf16[4,1152]{1,0:T(4,128)(2,1)S(1)}, bf16[4,1152]{1,0:T(4,128)(2,1)S(1)}, u32[]{:S(2)}, u32[]{:S(2)}) collective-permute-start(bf16[4,1152]{1,0:T(4,128)(2,1)S(1)} %pad_maximum_fusion.refs_0_), channel_id=1, source_target_pairs={{4,0},{0,4},{12,8},{8,12},{20,16},{16,20},{28,24},{24,28},{5,1},{1... | collective-permute-start | bytes 27656 | tf_op jit(solution)/shard_map/ppermute | solution.py:54
  15.2 4.2 %collective-permute-start.7 = (bf16[24,1152]{1,0:T(8,128)(2,1)S(1)}, bf16[24,1152]{1,0:T(8,128)(2,1)S(1)}, u32[]{:S(2)}, u32[]{:S(2)}) collective-permute-start(bf16[24,1152]{1,0:T(8,128)(2,1)S(1)} %shard_map.80.refs_3_), channel_id=1, source_target_pairs={{3,0},{2,1},{1,2},{0,3},{7,4},{6,5},{5,6},{4,7},{11,8},{10,9},{9,1... | collective-permute-start | bytes 165896 | tf_op jit(solution)/shard_map/ppermute | solution.py:290
  15.3 5.3 %collective-permute-start.8 = (bf16[24,1152]{1,0:T(8,128)(2,1)S(1)}, bf16[24,1152]{1,0:T(8,128)(2,1)S(1)}, u32[]{:S(2)}, u32[]{:S(2)}) collective-permute-start(bf16[24,1152]{1,0:T(8,128)(2,1)S(1)} %shard_map.80.refs_3_), channel_id=1, source_target_pairs={{2,0},{3,1},{0,2},{1,3},{6,4},{7,5},{4,6},{5,7},{10,8},{11,9},{8,1... | collective-permute-start | bytes 165896 | tf_op jit(solution)/shard_map/ppermute | solution.py:290
  16.9 3.7 %collective-permute-start.9 = (bf16[24,1152]{1,0:T(8,128)(2,1)S(1)}, bf16[24,1152]{1,0:T(8,128)(2,1)S(1)}, u32[]{:S(2)}, u32[]{:S(2)}) collective-permute-start(bf16[24,1152]{1,0:T(8,128)(2,1)S(1)} %shard_map.80.refs_3_), channel_id=1, source_target_pairs={{1,0},{0,1},{3,2},{2,3},{5,4},{4,5},{7,6},{6,7},{9,8},{8,9},{11,10... | collective-permute-start | bytes 165896 | tf_op jit(solution)/shard_map/ppermute | solution.py:290

commit v4 on v3

--- a/solution.py
+++ b/solution.py
@@ -143,14 +143,30 @@
     share[...] = dot(pooled_heads, w_out[...])
 
 
-def average(member, patch_rows, patch_mean):
+def average(lanes, devices, texts_here, member, chosen, share, patch_rows, pooled, label, order):
     belongs = member[...]
     count = jnp.sum(belongs, axis=1, keepdims=True)
-    patch_mean[...] = dot(belongs.astype(BF16), patch_rows[...], LAST_LAST) / count
+    patch_mean = dot(belongs.astype(BF16), patch_rows[...], LAST_LAST) / count
+    pooled[...] = patch_mean + share[...]
+
+    dp_index = lax.axis_index("dp")
+    mp_index = lax.axis_index("mp")
+    images, texts = label.shape
+    group = devices * texts_here
+    image_id = dp_index * images + iota((images, texts), 0)
+    index = iota((images, texts), 1)
+    text_dp = moved(dp_index, index % group // texts_here, digits_of(devices))
+    text_mp = moved(mp_index, index // group, digits_of(lanes))
+    text_id = (text_dp * lanes + text_mp) * texts_here + index % texts_here
+    label[...] = jnp.where(image_id == text_id, 1.0, -1.0)
+    goes = chosen[...]
+    for image in range(images):
+        order[image] = jnp.broadcast_to(goes[:, image : image + 1], order.shape[1:])
 
 
 def join(*refs):
     first, *texts, share, message = refs
+    texts[:2] = texts[1::-1]
     texts = [first, *texts[::-1]]
     text = jnp.concatenate([text[...].astype(F32) for text in texts], axis=0)
     text = text * lax.rsqrt(jnp.sum(text * text, axis=1, keepdims=True) + EPS)
@@ -158,43 +174,34 @@
 
 
 def pair(lanes, *refs):
-    chosen, patch_mean, share, own, *others, message = refs
+    pooled, label, order, own, *others, message = refs
     arrived = [own, *others[::-1]]
     devices = message.shape[0]
     dp_index = lax.axis_index("dp")
     mp_index = lax.axis_index("mp")
-    images, width = patch_mean.shape
+    images, width = pooled.shape
     group = arrived[0].shape[0] - images
     texts_here = group // devices
     slice_width = width // lanes
     part = message.shape[2] - width
 
-    pooled = patch_mean[...] + share[...]
+    total = pooled[...]
     for block in arrived[1:]:
-        pooled = pooled + block[...].astype(F32)[group:]
+        total = total + block[...].astype(F32)[group:]
     image_unit = (
-        pooled * lax.rsqrt(jnp.sum(pooled * pooled, axis=1, keepdims=True) + EPS)
+        total * lax.rsqrt(jnp.sum(total * total, axis=1, keepdims=True) + EPS)
     ).astype(BF16)
     text_unit = jnp.concatenate([block[:group] for block in arrived], axis=0)
-
-    def scaled(logits, image_dim, text_dim):
-        image_id = dp_index * images + iota(logits.shape, image_dim)
-        index = iota(logits.shape, text_dim)
-        text_dp = moved(dp_index, index % group // texts_here, digits_of(devices))
-        text_mp = moved(mp_index, index // group, digits_of(lanes))
-        text_id = (text_dp * lanes + text_mp) * texts_here + index % texts_here
-        label = jnp.where(image_id == text_id, 1.0, -1.0)
-        logits = 4.0 * logits - 2.0
-        return -4.0 * label * jax.nn.sigmoid(-label * logits)
 
     own_columns = text_unit[:, :slice_width]
     for lane in range(1, lanes):
         block = text_unit[:, lane * slice_width : (lane + 1) * slice_width]
         own_columns = jnp.where(mp_index == lane, block, own_columns)
-    by_image = scaled(dot(image_unit, text_unit, LAST_LAST), 0, 1)
+    signs = label[...]
+    logits = 4.0 * dot(image_unit, text_unit, LAST_LAST) - 2.0
+    by_image = -4.0 * signs * jax.nn.sigmoid(-signs * logits)
     text_grad = dot(by_image[:, :group].astype(BF16), image_unit, FIRST_FIRST)
-    goes = chosen[...]
-    rows = sum(goes[:, image : image + 1] * by_image[image : image + 1] for image in range(images))
+    rows = sum(order[image] * by_image[image : image + 1] for image in range(images))
     image_grad = dot(rows.astype(BF16), own_columns)
     parts = [image_grad[:, which * part : (which + 1) * part] for which in range(texts_here)]
     for position in range(devices):
@@ -278,13 +285,20 @@
         [patches_here, *pieces, bias, member, spread, w_qkv_here, w_out_here],
         scratch=[pltpu.VMEM((width, rows), F32)],
     )
-    patch_mean = call(
-        average,
-        shape((images, width), F32),
-        [member, patch_rows],
+    total = images * devices
+    pooled, label, order = call(
+        functools.partial(average, lanes, devices, texts_here),
+        (
+            shape((images, width), F32),
+            shape((images, total), F32),
+            shape((images, devices, total), F32),
+        ),
+        [member, chosen, share, patch_rows],
         cost=pl.CostEstimate(flops=10**9, bytes_accessed=0, transcendentals=0),
     )
-    texts = [texts[0], *texts[:0:-1]]
+    others = texts[:0:-1]
+    others[:2] = others[1::-1]
+    texts = [texts[0], *others]
     message = call(join, shape((devices * texts_here + images, width), BF16), [*texts, share])
     arrived = [message] + [
         lax.ppermute(message, "mp", [(moved(i, offset, mp_digits), i) for i in range(lanes)])
@@ -293,7 +307,7 @@
     message = call(
         functools.partial(pair, lanes),
         shape((devices, texts_here, width + slice_width // texts_here), BF16),
-        [chosen, patch_mean, share, arrived[0], *arrived[:0:-1]],
+        [pooled, label, order, arrived[0], *arrived[:0:-1]],
     )
     message = lax.all_to_all(message, "dp", split_axis=0, concat_axis=0, tiled=True)
     return call(

time: 32 us -> 32 us (level)
  no operation moved by 1% of the time
where the time goes in v4:
time: 32 us; the launch traced here: 31.8 us
  starting transfers between devices  11.4 us (36%)
  blocking collectives  9.91 us (31%)
  Pallas kernels  5.06 us (16%)
  waiting for transfers between devices  4.68 us (15%)
  between operations  0.69 us (2%)
    all_to_all x1, blocking collectives, on_device(): lax.all_to_all(message, 'dp', split_axis=0, concat_axis=0, tiled=True)  9.91 us
    ppermute x4, starting transfers between devices, fetch(): lax.ppermute(block, axis, [(shifted(i, stride, radix, by), i) for i in ra...  7.66 us
    pallas_call x6, Pallas kernels, call(): pl.pallas_call(kernel, out_shape=out_shape, in_specs=[pl.BlockSpec(memory...  5.06 us
    ppermute x3, waiting for transfers between devices, on_device(): lax.ppermute(message, 'mp', [(moved(i, offset, mp_digits), i) for i in ra...  3.24 us
    ppermute x3, starting transfers between devices, on_device(): lax.ppermute(message, 'mp', [(moved(i, offset, mp_digits), i) for i in ra...  1.92 us
    ppermute x3, starting transfers between devices, on_device(): lax.ppermute(patches, 'mp', [(moved(i, offset, mp_digits), i) for i in ra...  1.86 us
    ppermute x4, waiting for transfers between devices, fetch(): lax.ppermute(block, axis, [(shifted(i, stride, radix, by), i) for i in ra...  1.44 us
  transfers between devices with their start and end apart: 10, of which 4 were waited for; matrix products, arithmetic and copies ran while one was open for 0% of the time, Pallas kernels for 12%

profile of v4, /device:TPU:0, one launch (start us, length us, event | category | flops | bytes accessed | tf_op | source)
XLA Modules:
  0.0 31.8 jit_solution(18004444770495829644)
XLA Ops:
  0.6 4.1 %collective-permute-start.3 = (bf16[2,1152]{1,0:T(2,128)(2,1)}, bf16[2,1152]{1,0:T(2,128)(2,1)S(1)}, u32[]{:S(2)}, u32[]{:S(2)}) collective-permute-start(bf16[2,1152]{1,0:T(2,128)(2,1)} %refs_5_.1), channel_id=1, source_target_pairs={{16,0},{20,4},{24,8},{28,12},{0,16},{4,20},{8,24},{12,28},{17,1},{... | collective-permute-start | bytes 13832 | tf_op jit(solution)/shard_map/ppermute | solution.py:54
  4.7 0.0 collective-permute-start
  4.7 1.5 %collective-permute-start.1 = (bf16[288,128]{1,0:T(8,128)(2,1)}, bf16[288,128]{1,0:T(8,128)(2,1)S(1)}, u32[]{:S(2)}, u32[]{:S(2)}) collective-permute-start(bf16[288,128]{1,0:T(8,128)(2,1)} %refs_2_.1), channel_id=1, source_target_pairs={{2,0},{3,1},{0,2},{1,3},{6,4},{7,5},{4,6},{5,7},{10,8},{11,9},{8,1... | collective-permute-start | bytes 221192 | tf_op jit(solution)/shard_map/ppermute | solution.py:273
  6.2 0.4 %collective-permute-start.2 = (bf16[288,128]{1,0:T(8,128)(2,1)}, bf16[288,128]{1,0:T(8,128)(2,1)S(1)}, u32[]{:S(2)}, u32[]{:S(2)}) collective-permute-start(bf16[288,128]{1,0:T(8,128)(2,1)} %refs_2_.1), channel_id=1, source_target_pairs={{3,0},{2,1},{1,2},{0,3},{7,4},{6,5},{5,6},{4,7},{11,8},{10,9},{9,1... | collective-permute-start | bytes 221192 | tf_op jit(solution)/shard_map/ppermute | solution.py:273
  6.6 1.8 %shard_map.77 = (bf16[288,128]{1,0:T(8,128)(2,1)S(1)}, bf16[3,288,1152]{2,1,0:T(8,128)(2,1)S(1)}, bf16[288,1152]{1,0:T(8,128)(2,1)S(1)}, bf16[2,1152]{1,0:T(2,12...) custom-call(s32[64]{0:T(128)} %refs_0_.1, ...), custom_call_target="tpu_custom_call" | custom-call | bytes 5971968 | tf_op jit(solution)/shard_map/pallas_call | solution.py:228
  8.4 0.0 collective-permute-done.3
  8.4 1.6 %collective-permute-start.4 = (bf16[4,1152]{1,0:T(4,128)(2,1)S(1)}, bf16[4,1152]{1,0:T(4,128)(2,1)S(1)}, u32[]{:S(2)}, u32[]{:S(2)}) collective-permute-start(bf16[4,1152]{1,0:T(4,128)(2,1)S(1)} %pad_maximum_fusion.refs_0_), channel_id=1, source_target_pairs={{8,0},{12,4},{0,8},{4,12},{24,16},{28,20},{16,24},{20,28},{9,1},{1... | collective-permute-start | bytes 27656 | tf_op jit(solution)/shard_map/ppermute | solution.py:54
  10.1 1.4 %collective-permute-start.5 = (bf16[4,1152]{1,0:T(4,128)(2,1)S(1)}, bf16[4,1152]{1,0:T(4,128)(2,1)S(1)}, u32[]{:S(2)}, u32[]{:S(2)}) collective-permute-start(bf16[4,1152]{1,0:T(4,128)(2,1)S(1)} %pad_maximum_fusion.refs_0_), channel_id=1, source_target_pairs={{12,0},{8,4},{4,8},{0,12},{28,16},{24,20},{20,24},{16,28},{13,1},{... | collective-permute-start | bytes 27656 | tf_op jit(solution)/shard_map/ppermute | solution.py:54
  11.5 0.0 collective-permute-done.refs_1_
  11.5 0.5 %collective-permute-start.6 = (bf16[4,1152]{1,0:T(4,128)(2,1)S(1)}, bf16[4,1152]{1,0:T(4,128)(2,1)S(1)}, u32[]{:S(2)}, u32[]{:S(2)}) collective-permute-start(bf16[4,1152]{1,0:T(4,128)(2,1)S(1)} %pad_maximum_fusion.refs_0_), channel_id=1, source_target_pairs={{4,0},{0,4},{12,8},{8,12},{20,16},{16,20},{28,24},{24,28},{5,1},{1... | collective-permute-start | bytes 27656 | tf_op jit(solution)/shard_map/ppermute | solution.py:54
  12.0 0.0 collective-permute-done.1.refs_2_
  12.0 0.0 collective-permute-done.2.refs_3_
  12.0 1.7 %shard_map.78 = (f32[8,1152]{1,0:T(8,128)S(1)}, bf16[1152,128]{1,0:T(8,128)(2,1)S(1)}) custom-call(bf16[288,128]{1,0:T(8,128)(2,1)S(1)} %get-tuple-element.17.refs_0_, bf16[288,128]{1,0:T(8,128)(2,1)S(1)} %collective-permute-done.refs_1_, bf16[288,128]{1,0:T(8,128)(2,1)S(1)} %collective-permute-done.1.refs_2_, ...), custom_call_target="tpu_custom_call" | custom-call | tf_op jit(solution)/shard_map/pallas_call | solution.py:228
  13.7 0.0 collective-permute-done.4.refs_1_
  13.7 0.9 %collective-permute-done.5.refs_2_ = bf16[4,1152]{1,0:T(4,128)(2,1)S(1)} collective-permute-done((bf16[4,1152]{1,0:T(4,128)(2,1)S(1)}, bf16[4,1152]{1,0:T(4,128)(2,1)S(1)}, u32[]{:S(2)}, u32[]{:S(2)}) %collective-permute-start.5) | collective-permute-done | bytes 9248 | tf_op jit(solution)/shard_map/ppermute | solution.py:54
  14.6 0.5 %collective-permute-done.6.refs_3_ = bf16[4,1152]{1,0:T(4,128)(2,1)S(1)} collective-permute-done((bf16[4,1152]{1,0:T(4,128)(2,1)S(1)}, bf16[4,1152]{1,0:T(4,128)(2,1)S(1)}, u32[]{:S(2)}, u32[]{:S(2)}) %collective-permute-start.6) | collective-permute-done | bytes 9248 | tf_op jit(solution)/shard_map/ppermute | solution.py:54
  15.1 0.1 shard_map.80.refs_3_
  15.2 0.1 collective-permute-start.7
  15.3 1.6 %collective-permute-start.8 = (bf16[24,1152]{1,0:T(8,128)(2,1)S(1)}, bf16[24,1152]{1,0:T(8,128)(2,1)S(1)}, u32[]{:S(2)}, u32[]{:S(2)}) collective-permute-start(bf16[24,1152]{1,0:T(8,128)(2,1)S(1)} %shard_map.80.refs_3_), channel_id=1, source_target_pairs={{2,0},{3,1},{0,2},{1,3},{6,4},{7,5},{4,6},{5,7},{10,8},{11,9},{8,1... | collective-permute-start | bytes 165896 | tf_op jit(solution)/shard_map/ppermute | solution.py:304
  16.9 0.3 collective-permute-start.9
  17.2 0.2 shard_map.79
  17.4 2.0 %collective-permute-done.7.refs_4_ = bf16[24,1152]{1,0:T(8,128)(2,1)S(1)} collective-permute-done((bf16[24,1152]{1,0:T(8,128)(2,1)S(1)}, bf16[24,1152]{1,0:T(8,128)(2,1)S(1)}, u32[]{:S(2)}, u32[]{:S(2)}) %collective-permute-start.7) | collective-permute-done | bytes 55328 | tf_op jit(solution)/shard_map/ppermute | solution.py:304
  19.4 1.2 %collective-permute-done.8.refs_5_ = bf16[24,1152]{1,0:T(8,128)(2,1)S(1)} collective-permute-done((bf16[24,1152]{1,0:T(8,128)(2,1)S(1)}, bf16[24,1152]{1,0:T(8,128)(2,1)S(1)}, u32[]{:S(2)}, u32[]{:S(2)}) %collective-permute-start.8) | collective-permute-done | bytes 55328 | tf_op jit(solution)/shard_map/ppermute | solution.py:304
  20.6 0.0 collective-permute-done.9.refs_6_
  20.6 0.6 %shard_map.81 = bf16[8,2,1296]{2,1,0:T(2,128)(2,1)S(1)} custom-call(f32[8,1152]{1,0:T(8,128)S(1)} %get-tuple-element.24.refs_0_, f32[8,64]{1,0:T(8,128)S(1)} %get-tuple-element.25.refs_1_, f32[8,8,64]{2,1,0:T(8,128)S(1)} %get-tuple-element.26.refs_2_, bf16[24,1152]{1,0:T(8,128)(2,1)S(1)} %shard_map.80.refs_3_, ...), custom_call_target="tpu_custom_call" | custom-call | tf_op jit(solution)/shard_map/pallas_call | solution.py:228
  21.2 9.9 %all_to_all.5.message = bf16[8,2,1296]{2,1,0:T(2,128)(2,1)S(1)} all-to-all(bf16[8,2,1296]{2,1,0:T(2,128)(2,1)S(1)} %shard_map.81), channel_id=1, replica_groups=mesh['dp'=8,'mp'=4] {'dp'}, dimensions={0} | all-to-all | bytes 82944 | tf_op jit(solution)/shard_map/all_to_all | solution.py:312
  31.1 0.7 %shard_map.82 = (f32[8,288]{1,0:T(8,128)}, f32[2,1152]{1,0:T(2,128)}) custom-call(bf16[8,2,1296]{2,1,0:T(2,128)(2,1)S(1)} %all_to_all.5.message), custom_call_target="tpu_custom_call" | custom-call | tf_op jit(solution)/shard_map/pallas_call | solution.py:228
  (1 shorter events, 0.0 us)
Async XLA Ops:
  0.6 7.8 %collective-permute-start.3 = (bf16[2,1152]{1,0:T(2,128)(2,1)}, bf16[2,1152]{1,0:T(2,128)(2,1)S(1)}, u32[]{:S(2)}, u32[]{:S(2)}) collective-permute-start(bf16[2,1152]{1,0:T(2,128)(2,1)} %refs_5_.1), channel_id=1, source_target_pairs={{16,0},{20,4},{24,8},{28,12},{0,16},{4,20},{8,24},{12,28},{17,1},{... | collective-permute-start | bytes 13832 | tf_op jit(solution)/shard_map/ppermute | solution.py:54
  4.7 6.7 %collective-permute-start = (bf16[288,128]{1,0:T(8,128)(2,1)}, bf16[288,128]{1,0:T(8,128)(2,1)S(1)}, u32[]{:S(2)}, u32[]{:S(2)}) collective-permute-start(bf16[288,128]{1,0:T(8,128)(2,1)} %refs_2_.1), channel_id=1, source_target_pairs={{1,0},{0,1},{3,2},{2,3},{5,4},{4,5},{7,6},{6,7},{9,8},{8,9},{11,10... | collective-permute-start | bytes 221192 | tf_op jit(solution)/shard_map/ppermute | solution.py:273
  4.7 7.2 %collective-permute-start.1 = (bf16[288,128]{1,0:T(8,128)(2,1)}, bf16[288,128]{1,0:T(8,128)(2,1)S(1)}, u32[]{:S(2)}, u32[]{:S(2)}) collective-permute-start(bf16[288,128]{1,0:T(8,128)(2,1)} %refs_2_.1), channel_id=1, source_target_pairs={{2,0},{3,1},{0,2},{1,3},{6,4},{7,5},{4,6},{5,7},{10,8},{11,9},{8,1... | collective-permute-start | bytes 221192 | tf_op jit(solution)/shard_map/ppermute | solution.py:273
  6.2 5.8 %collective-permute-start.2 = (bf16[288,128]{1,0:T(8,128)(2,1)}, bf16[288,128]{1,0:T(8,128)(2,1)S(1)}, u32[]{:S(2)}, u32[]{:S(2)}) collective-permute-start(bf16[288,128]{1,0:T(8,128)(2,1)} %refs_2_.1), channel_id=1, source_target_pairs={{3,0},{2,1},{1,2},{0,3},{7,4},{6,5},{5,6},{4,7},{11,8},{10,9},{9,1... | collective-permute-start | bytes 221192 | tf_op jit(solution)/shard_map/ppermute | solution.py:273
  8.4 5.3 %collective-permute-start.4 = (bf16[4,1152]{1,0:T(4,128)(2,1)S(1)}, bf16[4,1152]{1,0:T(4,128)(2,1)S(1)}, u32[]{:S(2)}, u32[]{:S(2)}) collective-permute-start(bf16[4,1152]{1,0:T(4,128)(2,1)S(1)} %pad_maximum_fusion.refs_0_), channel_id=1, source_target_pairs={{8,0},{12,4},{0,8},{4,12},{24,16},{28,20},{16,24},{20,28},{9,1},{1... | collective-permute-start | bytes 27656 | tf_op jit(solution)/shard_map/ppermute | solution.py:54
  10.1 4.6 %collective-permute-start.5 = (bf16[4,1152]{1,0:T(4,128)(2,1)S(1)}, bf16[4,1152]{1,0:T(4,128)(2,1)S(1)}, u32[]{:S(2)}, u32[]{:S(2)}) collective-permute-start(bf16[4,1152]{1,0:T(4,128)(2,1)S(1)} %pad_maximum_fusion.refs_0_), channel_id=1, source_target_pairs={{12,0},{8,4},{4,8},{0,12},{28,16},{24,20},{20,24},{16,28},{13,1},{... | collective-permute-start | bytes 27656 | tf_op jit(solution)/shard_map/ppermute | solution.py:54
  11.5 3.7 %collective-permute-start.6 = (bf16[4,1152]{1,0:T(4,128)(2,1)S(1)}, bf16[4,1152]{1,0:T(4,128)(2,1)S(1)}, u32[]{:S(2)}, u32[]{:S(2)}) collective-permute-start(bf16[4,1152]{1,0:T(4,128)(2,1)S(1)} %pad_maximum_fusion.refs_0_), channel_id=1, source_target_pairs={{4,0},{0,4},{12,8},{8,12},{20,16},{16,20},{28,24},{24,28},{5,1},{1... | collective-permute-start | bytes 27656 | tf_op jit(solution)/shard_map/ppermute | solution.py:54
  15.2 4.2 %collective-permute-start.7 = (bf16[24,1152]{1,0:T(8,128)(2,1)S(1)}, bf16[24,1152]{1,0:T(8,128)(2,1)S(1)}, u32[]{:S(2)}, u32[]{:S(2)}) collective-permute-start(bf16[24,1152]{1,0:T(8,128)(2,1)S(1)} %shard_map.80.refs_3_), channel_id=1, source_target_pairs={{3,0},{2,1},{1,2},{0,3},{7,4},{6,5},{5,6},{4,7},{11,8},{10,9},{9,1... | collective-permute-start | bytes 165896 | tf_op jit(solution)/shard_map/ppermute | solution.py:304
  15.3 5.3 %collective-permute-start.8 = (bf16[24,1152]{1,0:T(8,128)(2,1)S(1)}, bf16[24,1152]{1,0:T(8,128)(2,1)S(1)}, u32[]{:S(2)}, u32[]{:S(2)}) collective-permute-start(bf16[24,1152]{1,0:T(8,128)(2,1)S(1)} %shard_map.80.refs_3_), channel_id=1, source_target_pairs={{2,0},{3,1},{0,2},{1,3},{6,4},{7,5},{4,6},{5,7},{10,8},{11,9},{8,1... | collective-permute-start | bytes 165896 | tf_op jit(solution)/shard_map/ppermute | solution.py:304
  16.9 3.7 %collective-permute-start.9 = (bf16[24,1152]{1,0:T(8,128)(2,1)S(1)}, bf16[24,1152]{1,0:T(8,128)(2,1)S(1)}, u32[]{:S(2)}, u32[]{:S(2)}) collective-permute-start(bf16[24,1152]{1,0:T(8,128)(2,1)S(1)} %shard_map.80.refs_3_), channel_id=1, source_target_pairs={{1,0},{0,1},{3,2},{2,3},{5,4},{4,5},{7,6},{6,7},{9,8},{8,9},{11,10... | collective-permute-start | bytes 165896 | tf_op jit(solution)/shard_map/ppermute | solution.py:304
